TPU v7x, 32 devices: a whole 2x2x4 slice. The times are simulated.
32 devices in a mesh: ctx: 16 (over z, y, x), wt: 2 (over core).
Axes of the slice: x: 2, y: 2, z: 4, core: 2. Of those that a mesh axis runs over, the one named last changes fastest.
Arguments:
- tokens: bfloat16 [2, 4096, 1024], P('wt', 'ctx'), may hold values from -6 to 6
- block_table: int32 [16, 2], P('ctx'), may hold values from 0 to 31, as said below
- doc_flags: int32 [2, 4096], P('wt', 'ctx'), may hold values from 0 to 1, as said below
- w_query: float32 [1024, 1024], P(('ctx', 'wt')), may hold values from -0.1875 to 0.1875
- key_weight: float32 [1024, 512], P(('ctx', 'wt')), may hold values from -0.1875 to 0.1875
- value_weight: float32 [1024, 512], P(('ctx', 'wt')), may hold values from -0.1875 to 0.1875
- w_out: float32 [1024, 1024], P(('ctx', 'wt')), may hold values from -2 to 2
- w_gate: float32 [1024, 4608], P(('ctx', 'wt')), may hold values from -0.1875 to 0.1875
- w_up: float32 [1024, 4608], P(('ctx', 'wt')), may hold values from -0.1875 to 0.1875
- w_down: float32 [1024, 4608], P(('ctx', 'wt')), may hold values from -0.09375 to 0.09375
- gain_attn: float32 [1024], P(('ctx', 'wt')), may hold values from 0.25 to 1.75
- gain_mlp: float32 [1024], P(('ctx', 'wt')), may hold values from 0.25 to 1.75
- gain_q: float32 [64], replicated, may hold values from 0.25 to 1.75
- key_norm_gain: float32 [64], replicated, may hold values from 0.25 to 1.75
- cotangent: bfloat16 [2, 4096, 1024], P('wt', 'ctx'), may hold values from -6 to 6
Outputs:
- layer_out: bfloat16 [2, 4096, 1024], P('wt', 'ctx')
- grad_input: float32 [2, 4096, 1024], P('wt', 'ctx')
- grad_query: float32 [1024, 1024], P(('ctx', 'wt'))
- grad_key: float32 [1024, 512], P(('ctx', 'wt'))
- grad_value: float32 [1024, 512], P(('ctx', 'wt'))
- grad_wout: float32 [1024, 1024], P(('ctx', 'wt'))
- grad_gate: float32 [1024, 4608], P(('ctx', 'wt'))
- grad_up: float32 [1024, 4608], P(('ctx', 'wt'))
- grad_down: float32 [1024, 4608], P(('ctx', 'wt'))
- grad_gattn: float32 [1024], P(('ctx', 'wt'))
- grad_gmlp: float32 [1024], P(('ctx', 'wt'))
- grad_gq: float32 [64], replicated
- grad_gk: float32 [64], replicated
Inputs may be any that keep to these rules, and one draw needn't show every extreme that they name: `block_table`: row c names the two blocks held at index c of ctx: a block p under 16, then 2 * 16 - 1 - p; every block of a sequence appears once; block b covers positions b * 128 to (b + 1) * 128 - 1. `doc_flags`: rows in the same order as tokens; the token at position 0 of each sequence always begins a document.
All inputs are finite; a program needn't handle non-finite values.
Results may differ from a plain program's by a relative error of at most 0.04.
Values may be sent and summed in bfloat16 or wider, within the bound.
No kernel may reach another device: no remote copies, remote signals or barrier semaphores. Data moves between devices by JAX's collectives and lax.ppermute only.
A program may use at most 320 MiB of HBM per device.

v0:
```python
import functools

import jax
import jax.numpy as jnp
import numpy as np
from jax import lax
from jax.experimental import pallas as pl
from jax.experimental.pallas import tpu as pltpu
from jax.sharding import PartitionSpec as P

HEADS = 16
KV_HEADS = 8
HEAD = 64
LANES = 2 * HEAD
BLOCK = 128
EPS = 1e-05
SCALE = HEAD**-0.5
BF = jnp.bfloat16
F32 = jnp.float32
I32 = jnp.int32
QT = 512
KT = 512
VMEM_BYTES = 56 * 1024 * 1024

NN = (((1,), (0,)), ((), ()))
NT = (((1,), (1,)), ((), ()))
TN = (((0,), (0,)), ((), ()))


def dot(a, b, dims=NN):
    return lax.dot_general(a, b, dims, preferred_element_type=F32)


def params(**kw):
    return pltpu.CompilerParams(vmem_limit_bytes=VMEM_BYTES, **kw)


def in_vmem():
    return pl.BlockSpec(memory_space=pltpu.VMEM)


def in_smem():
    return pl.BlockSpec(memory_space=pltpu.SMEM)


def low_lanes(shape):
    return lax.broadcasted_iota(I32, shape, 1) < HEAD


def half_sums(value, low):
    total = jnp.sum(value, axis=-1, keepdims=True)
    first = jnp.sum(jnp.where(low, value, 0.0), axis=-1, keepdims=True)
    return jnp.where(low, first, total - first)


def half_turn(value):
    lane = lax.broadcasted_iota(I32, value.shape, 1)
    first = (lane % HEAD) < HEAD // 2
    return jnp.where(
        first,
        pltpu.roll(value, LANES - HEAD // 2, 1),
        pltpu.roll(value, HEAD // 2, 1),
    )


def project_kernel(n_parts, swaps, core_ref, x_ref, norm_gain_ref, gain_ref, cos_ref, sin_ref, *refs):
    weights, (n_ref, raw_ref, out_ref) = refs[: 2 * n_parts], refs[2 * n_parts :]
    rows = cos_ref.shape[0]
    is_value = core_ref[0] == 1
    x = x_ref[...].astype(F32)
    inverse = lax.rsqrt(jnp.mean(x * x, axis=-1, keepdims=True) + EPS)
    n_ref[...] = (x * inverse * norm_gain_ref[...]).astype(BF)
    groups = KV_HEADS // 2
    for half in range(2):
        total, at = None, 0
        for part in weights[half * n_parts : (half + 1) * n_parts]:
            length = part.shape[0]
            pieces = [n_ref[:, e : e + swaps[2]] for e in swaps[half][at // swaps[2] : (at + length) // swaps[2]]]
            left = pieces[0] if len(pieces) == 1 else jnp.concatenate(pieces, axis=1)
            term = dot(left, part[:, : groups * LANES])
            total = term if total is None else total + term
            at += length
        raw_ref[:, half * groups * LANES : (half + 1) * groups * LANES] = total
    low = low_lanes((rows, LANES))
    turns = jnp.logical_or(low, jnp.logical_not(is_value))
    for g in range(KV_HEADS):
        for s in range(2):
            raw = raw_ref[s * rows : (s + 1) * rows, g * LANES : (g + 1) * LANES]
            inverse = lax.rsqrt(half_sums(raw * raw, low) * (1.0 / HEAD) + EPS)
            normed = raw * inverse * gain_ref[...]
            turned = normed * cos_ref[...] + half_turn(normed) * sin_ref[...]
            out_ref[g, s] = jnp.where(turns, turned, raw).astype(BF)


def project(core, x, norm_gain, gain, cosine, sine, parts, chunk, chunk_orders):
    rows = cosine.shape[0]
    n_parts = len(parts[0])
    swaps = ([c * chunk for c in chunk_orders[0]], [c * chunk for c in chunk_orders[1]], chunk)
    return pl.pallas_call(
        functools.partial(project_kernel, n_parts, swaps),
        in_specs=[in_smem()] + [in_vmem()] * (5 + 2 * n_parts),
        out_specs=[in_vmem()] * 3,
        out_shape=[
            jax.ShapeDtypeStruct(x.shape, BF),
            jax.ShapeDtypeStruct((2 * rows, KV_HEADS * LANES), F32),
            jax.ShapeDtypeStruct((KV_HEADS, 2, rows, LANES), BF),
        ],
        compiler_params=params(),
        cost_estimate=pl.CostEstimate(flops=2 * x.shape[0] * x.shape[1] * KV_HEADS * LANES, bytes_accessed=8 << 20, transcendentals=0),
    )(core, x, norm_gain, gain, cosine, sine, *parts[0], *parts[1])


def unproject_kernel(core_ref, grad_ref, raw_ref, gain_ref, cos_ref, sin_ref, out_ref, gain_out_ref):
    rows = cos_ref.shape[0]
    is_value = core_ref[0] == 1
    for s in range(2):
        raw = raw_ref[s * rows : (s + 1) * rows]
        grad = grad_ref[0, s].astype(F32)
        low = low_lanes(raw.shape)
        inverse = lax.rsqrt(half_sums(raw * raw, low) * (1.0 / HEAD) + EPS)
        back = grad * cos_ref[...] + half_turn(grad * sin_ref[...])
        is_q_or_k = jnp.logical_or(low, jnp.logical_not(is_value))
        gain_rows = jnp.sum(back * raw * inverse, axis=0, keepdims=True)
        scaled = back * gain_ref[...]
        mean = half_sums(scaled * raw, low) * (1.0 / HEAD)
        moved = inverse * scaled - raw * (inverse * inverse * inverse) * mean
        out_ref[s * rows : (s + 1) * rows, :] = jnp.where(is_q_or_k, moved, grad).astype(BF)
        gain_rows = jnp.where(is_q_or_k[:1], gain_rows, 0.0)
        if s == 0:
            total = gain_rows
        else:
            total = total + gain_rows
    gain_out_ref[0] = jnp.broadcast_to(total, (8, LANES))


def unproject(core, grads, raw, gain, cosine, sine):
    rows = cosine.shape[0]
    return pl.pallas_call(
        unproject_kernel,
        grid=(KV_HEADS,),
        in_specs=[
            in_smem(),
            pl.BlockSpec((1, 2, rows, LANES), lambda g: (g, 0, 0, 0)),
            pl.BlockSpec((2 * rows, LANES), lambda g: (0, g)),
            pl.BlockSpec((1, LANES), lambda g: (0, 0)),
            pl.BlockSpec((rows, LANES), lambda g: (0, 0)),
            pl.BlockSpec((rows, LANES), lambda g: (0, 0)),
        ],
        out_specs=[
            pl.BlockSpec((2 * rows, LANES), lambda g: (0, g)),
            pl.BlockSpec((1, 8, LANES), lambda g: (g, 0, 0)),
        ],
        out_shape=[
            jax.ShapeDtypeStruct((2 * rows, KV_HEADS * LANES), BF),
            jax.ShapeDtypeStruct((KV_HEADS, 8, LANES), F32),
        ],
        compiler_params=params(),
        cost_estimate=pl.CostEstimate(flops=1 << 24, bytes_accessed=8 << 20, transcendentals=0),
    )(core, grads, raw, gain, cosine, sine)


def block_rows(ref, slot):
    return ref[pl.ds(pl.multiple_of(slot * BLOCK, BLOCK), BLOCK), :]


def sum_of_parts(value):
    first = value.astype(BF)
    rest = value - first.astype(F32)
    second = rest.astype(BF)
    third = (rest - second.astype(F32)).astype(BF)
    return first, second, third


def allowed_pairs(j, pos_row, start_row):
    key_pos = j * KT + lax.broadcasted_iota(I32, (KT, 1), 0)
    return jnp.logical_and(key_pos <= pos_row, key_pos >= start_row)


def walk_keys(lims_ref, i, step, carry):
    lo, full_lo, full_hi, hi = (lims_ref[e, i] for e in range(4))
    carry = lax.fori_loop(lo, full_lo, functools.partial(step, True), carry)
    carry = lax.fori_loop(full_lo, full_hi, functools.partial(step, False), carry)
    return lax.fori_loop(full_hi, hi, functools.partial(step, True), carry)


def attend_kernel(
    core_ref, kslot_ref, qslot_ref, lims_ref, q_ref, own_ref, other_ref, pos_ref, start_ref,
    out_ref, keep_ref, lse_ref, keys, values_t, placed,
):
    q_tiles = q_ref.shape[0] // QT
    k_tiles = own_ref.shape[0] // KT
    per = KT // BLOCK
    is_first = core_ref[0] == 0
    values_t[HEAD:, :] = jnp.ones((values_t.shape[0] - HEAD, values_t.shape[1]), BF)

    def load(t, carry):
        for b in range(per):
            slot = kslot_ref[t * per + b]
            own = block_rows(own_ref, slot)[:, HEAD:]
            other = block_rows(other_ref, slot)[:, HEAD:]
            at = pl.ds(pl.multiple_of((t * per + b) * BLOCK, BLOCK), BLOCK)
            keys[at, :] = jnp.where(is_first, own, other)
            value = jnp.where(is_first, other, own).astype(F32)
            values_t[:HEAD, at] = value.T.astype(BF)
        return carry

    lax.fori_loop(0, k_tiles, load, 0)

    def tile(i, carry):
        cols = pl.ds(pl.multiple_of(i * QT, QT), QT)
        parts = [block_rows(q_ref, qslot_ref[i * (QT // BLOCK) + b])[:, :HEAD] for b in range(QT // BLOCK)]
        query_t = (jnp.concatenate(parts, axis=0).astype(F32) * SCALE).T.astype(BF)
        pos_row = pos_ref[:, cols]
        start_row = start_ref[:, cols]

        def step(masked, j, acc):
            at = pl.ds(pl.multiple_of(j * KT, KT), KT)
            p = jnp.exp(dot(keys[at, :], query_t))
            if masked:
                p = jnp.where(allowed_pairs(j, pos_row, start_row), p, 0.0)
            return acc + dot(values_t[:, at], p.astype(BF))

        acc = walk_keys(lims_ref, i, step, jnp.zeros((values_t.shape[0], QT), F32))
        total = acc[HEAD : HEAD + 1]
        mixed = acc[:HEAD] / total
        keep_ref[:, cols] = mixed
        lse_ref[:, cols] = jnp.log(total)
        rows = mixed.T
        for b in range(QT // BLOCK):
            slot = qslot_ref[i * (QT // BLOCK) + b]
            placed[pl.ds(pl.multiple_of(slot * BLOCK, BLOCK), BLOCK), :] = rows[b * BLOCK : (b + 1) * BLOCK]
        return carry

    lax.fori_loop(0, q_tiles, tile, 0)

    def pack(c, carry):
        first = placed[pl.ds(pl.multiple_of(c * 2 * BLOCK, BLOCK), BLOCK), :]
        second = placed[pl.ds(pl.multiple_of((c * 2 + 1) * BLOCK, BLOCK), BLOCK), :]
        out_ref[pl.ds(pl.multiple_of(c * BLOCK, BLOCK), BLOCK), :] = jnp.concatenate([first, second], axis=1).astype(BF)
        return carry

    lax.fori_loop(0, q_ref.shape[0] // (2 * BLOCK), pack, 0)


def attend(core, tables, queries, own, other):
    kslot, qslot, lims, pos, start = tables
    n_q, n_k = queries.shape[0], own.shape[0]
    return pl.pallas_call(
        attend_kernel,
        in_specs=[in_smem()] * 4 + [in_vmem()] * 5,
        out_specs=[in_vmem()] * 3,
        out_shape=[
            jax.ShapeDtypeStruct((n_q // 2, LANES), BF),
            jax.ShapeDtypeStruct((HEAD, n_q), F32),
            jax.ShapeDtypeStruct((1, n_q), F32),
        ],
        scratch_shapes=[
            pltpu.VMEM((n_k, HEAD), BF),
            pltpu.VMEM((HEAD + 16, n_k), BF),
            pltpu.VMEM((n_q, HEAD), F32),
        ],
        compiler_params=params(),
        cost_estimate=pl.CostEstimate(flops=8 * n_q * n_k * HEAD, bytes_accessed=8 << 20, transcendentals=n_q * n_k),
    )(core, kslot, qslot, lims, queries, own, other, pos, start)


def attend_back_kernel(
    core_ref, kslot_ref, qslot_ref, lims_ref, q_ref, own_ref, other_ref, pos_ref, start_ref,
    grad_ref, mixed_ref, lse_ref,
    dq_ref, keep_ref, send_ref,
    keys, values, keys_t, grad_keys, grad_values, grad_placed,
):
    q_tiles = q_ref.shape[0] // QT
    k_tiles = own_ref.shape[0] // KT
    per = KT // BLOCK
    is_first = core_ref[0] == 0
    ones = jnp.ones((BLOCK, HEAD), BF)

    def load(t, carry):
        for b in range(per):
            slot = kslot_ref[t * per + b]
            own = block_rows(own_ref, slot)[:, HEAD:]
            other = block_rows(other_ref, slot)[:, HEAD:]
            at = pl.ds(pl.multiple_of((t * per + b) * BLOCK, BLOCK), BLOCK)
            key = jnp.where(is_first, own, other)
            value = jnp.where(is_first, other, own)
            keys[at, :] = jnp.concatenate([key, ones], axis=1)
            values[at, :] = jnp.concatenate([value, ones], axis=1)
            keys_t[:, at] = key.astype(F32).T.astype(BF)
            grad_keys[at, :] = jnp.zeros((BLOCK, HEAD), F32)
            grad_values[at, :] = jnp.zeros((BLOCK, HEAD), F32)
        return carry

    lax.fori_loop(0, k_tiles, load, 0)

    def unpack(c, carry):
        pair = grad_ref[pl.ds(pl.multiple_of(c * BLOCK, BLOCK), BLOCK), :]
        grad_placed[pl.ds(pl.multiple_of(c * 2 * BLOCK, BLOCK), BLOCK), :] = pair[:, :HEAD]
        grad_placed[pl.ds(pl.multiple_of((c * 2 + 1) * BLOCK, BLOCK), BLOCK), :] = pair[:, HEAD:]
        return carry

    lax.fori_loop(0, q_ref.shape[0] // (2 * BLOCK), unpack, 0)

    def tile(i, carry):
        cols = pl.ds(pl.multiple_of(i * QT, QT), QT)
        slots = [qslot_ref[i * (QT // BLOCK) + b] for b in range(QT // BLOCK)]
        query_f = jnp.concatenate([block_rows(q_ref, s)[:, :HEAD] for s in slots], axis=0).astype(F32) * SCALE
        grad = jnp.concatenate([block_rows(grad_placed, s) for s in slots], axis=0)
        query = query_f.astype(BF)
        grad_t = grad.astype(F32).T
        delta = jnp.sum(grad_t * mixed_ref[:, cols], axis=0, keepdims=True)
        pad = jnp.zeros((HEAD - 3, QT), F32)
        query_t = jnp.concatenate(
            [query_f.T] + [e.astype(F32) for e in sum_of_parts(-lse_ref[:, cols])] + [pad], axis=0
        ).astype(BF)
        grad_t = jnp.concatenate([grad_t] + [e.astype(F32) for e in sum_of_parts(-delta)] + [pad], axis=0).astype(BF)
        pos_row = pos_ref[:, cols]
        start_row = start_ref[:, cols]

        def step(masked, j, acc):
            at = pl.ds(pl.multiple_of(j * KT, KT), KT)
            p = jnp.exp(dot(keys[at, :], query_t))
            if masked:
                p = jnp.where(allowed_pairs(j, pos_row, start_row), p, 0.0)
            grad_s = (p * dot(values[at, :], grad_t)).astype(BF)
            grad_values[at, :] += dot(p.astype(BF), grad)
            grad_keys[at, :] += dot(grad_s, query)
            return acc + dot(keys_t[:, at], grad_s)

        acc = walk_keys(lims_ref, i, step, jnp.zeros((HEAD, QT), F32))
        rows = (acc * SCALE).T
        rows = jnp.concatenate([rows, jnp.zeros((QT, HEAD), F32)], axis=1)
        for b in range(QT // BLOCK):
            dq_ref[pl.ds(pl.multiple_of(slots[b] * BLOCK, BLOCK), BLOCK), :] = rows[b * BLOCK : (b + 1) * BLOCK]
        return carry

    lax.fori_loop(0, q_tiles, tile, 0)

    def place(t, carry):
        zeros = jnp.zeros((BLOCK, HEAD), F32)
        for b in range(per):
            slot = kslot_ref[t * per + b]
            at = pl.ds(pl.multiple_of((t * per + b) * BLOCK, BLOCK), BLOCK)
            to = pl.ds(pl.multiple_of(slot * BLOCK, BLOCK), BLOCK)
            key, value = grad_keys[at, :], grad_values[at, :]
            mine = jnp.where(is_first, key, value)
            theirs = jnp.where(is_first, value, key)
            keep_ref[to, :] = jnp.concatenate([zeros, mine], axis=1)
            send_ref[to, :] = jnp.concatenate([zeros, theirs], axis=1).astype(BF)
        return carry

    lax.fori_loop(0, k_tiles, place, 0)


def attend_back(core, tables, queries, own, other, grads, mixed, lse):
    kslot, qslot, lims, pos, start = tables
    n_q, n_k = queries.shape[0], own.shape[0]
    return pl.pallas_call(
        attend_back_kernel,
        in_specs=[in_smem()] * 4 + [in_vmem()] * 8,
        out_specs=[in_vmem()] * 3,
        out_shape=[
            jax.ShapeDtypeStruct((n_q, LANES), F32),
            jax.ShapeDtypeStruct((n_k, LANES), F32),
            jax.ShapeDtypeStruct((n_k, LANES), BF),
        ],
        scratch_shapes=[
            pltpu.VMEM((n_k, LANES), BF),
            pltpu.VMEM((n_k, LANES), BF),
            pltpu.VMEM((HEAD, n_k), BF),
            pltpu.VMEM((n_k, HEAD), F32),
            pltpu.VMEM((n_k, HEAD), F32),
            pltpu.VMEM((n_q, HEAD), BF),
        ],
        compiler_params=params(),
        cost_estimate=pl.CostEstimate(flops=16 * n_q * n_k * HEAD, bytes_accessed=8 << 20, transcendentals=n_q * n_k),
    )(core, kslot, qslot, lims, queries, own, other, pos, start, grads, mixed, lse)


def columns_of(value, chunk, order, part, parts):
    count = len(order) // parts
    pieces = [value[:, e * chunk : (e + 1) * chunk] for e in order[part * count : (part + 1) * count]]
    return jnp.concatenate(pieces, axis=1)


def in_order(values, chunk, order):
    joined = jnp.concatenate(values, axis=1)
    places = sorted(range(len(order)), key=lambda e: order[e])
    return jnp.concatenate([joined[:, e * chunk : (e + 1) * chunk] for e in places], axis=1)


def feed_kernel(n_parts, chunk, orders, n_ref, c_ref, *refs):
    first, second = refs[:n_parts], refs[n_parts : 2 * n_parts]
    mid_ref, gate_ref, up_ref, out_ref, back_ref, nt_ref = refs[2 * n_parts :]
    quarter = mid_ref.shape[1]
    split = first[0].shape[1] - quarter
    normed, upstream = n_ref[...], c_ref[...]

    def over_parts(value, order, parts, lo, hi):
        total = None
        for p, part in enumerate(parts):
            term = dot(columns_of(value, chunk, order, p, n_parts), part[:, lo:hi])
            total = term if total is None else total + term
        return total

    gate = over_parts(normed, orders[0], first, 0, quarter)
    up = over_parts(normed, orders[1], second, 0, quarter)
    down = jnp.concatenate(
        [
            over_parts(upstream, orders[0], first, quarter, quarter + split),
            over_parts(upstream, orders[1], second, quarter, 2 * quarter - split),
        ],
        axis=1,
    )
    sig = 1.0 / (1.0 + jnp.exp(-gate))
    silu = gate * sig
    mid_ref[...] = (silu * up).astype(BF)
    gate_ref[...] = (down * up * (sig * (1.0 + gate * (1.0 - sig)))).astype(BF)
    up_ref[...] = (down * silu).astype(BF)
    out_ref[...] = in_order(
        [dot(mid_ref[:, :split], part[:, quarter:], NT) for part in first], chunk, orders[0]
    ) + in_order([dot(mid_ref[:, split:], part[:, quarter:], NT) for part in second], chunk, orders[1])
    back = in_order([dot(gate_ref[...], part[:, :quarter], NT) for part in first], chunk, orders[0]) + in_order(
        [dot(up_ref[...], part[:, :quarter], NT) for part in second], chunk, orders[1]
    )
    back_ref[...] = back.astype(BF)
    nt_ref[...] = normed.T


def feed(n, c, parts, chunk, orders, quarter):
    rows, width = n.shape
    step = rows // 2
    tall = lambda cols: pl.BlockSpec((step, cols), lambda i: (i, 0))
    whole = [p for piece in parts for p in piece]
    return pl.pallas_call(
        functools.partial(feed_kernel, len(parts[0]), chunk, orders),
        grid=(2,),
        in_specs=[tall(width)] * 2 + [pl.BlockSpec(p.shape, lambda i: (0, 0)) for p in whole],
        out_specs=[tall(quarter)] * 3 + [tall(width)] * 2 + [pl.BlockSpec((width, step), lambda i: (0, i))],
        out_shape=[jax.ShapeDtypeStruct((rows, quarter), BF)] * 3
        + [jax.ShapeDtypeStruct(e, t) for e, t in (((rows, width), F32), ((rows, width), BF), ((width, rows), BF))],
        compiler_params=params(),
        cost_estimate=pl.CostEstimate(flops=12 * rows * width * quarter, bytes_accessed=16 << 20, transcendentals=0),
    )(n, c, *whole)


def turn_kernel(a_ref, b_ref, a_out_ref, b_out_ref):
    a_out_ref[...] = a_ref[...].T
    b_out_ref[...] = b_ref[...].T


def turn(a, b):
    return pl.pallas_call(
        turn_kernel,
        in_specs=[in_vmem()] * 2,
        out_specs=[in_vmem()] * 2,
        out_shape=[jax.ShapeDtypeStruct(v.shape[::-1], v.dtype) for v in (a, b)],
        compiler_params=params(),
        cost_estimate=pl.CostEstimate(flops=1 << 20, bytes_accessed=4 << 20, transcendentals=0),
    )(a, b)


def out_grad_kernel(core_ref, attn_ref, grad_ref, select_ref, unperm_ref, out_ref):
    half = unperm_ref.shape[1] // 2
    rel = dot(attn_ref[...], select_ref[...]).astype(BF).T
    cols = jnp.where(core_ref[0] == 0, unperm_ref[:, :half], unperm_ref[:, half:])
    out_ref[...] = dot(rel, dot(grad_ref[...], cols).astype(BF)).astype(BF)


def out_grad(core, attn, grad, select, unperm):
    width = select.shape[0]
    return pl.pallas_call(
        out_grad_kernel,
        in_specs=[in_smem()] + [in_vmem()] * 4,
        out_specs=in_vmem(),
        out_shape=jax.ShapeDtypeStruct((width, width // 2), BF),
        compiler_params=params(),
        cost_estimate=pl.CostEstimate(flops=4 << 30, bytes_accessed=8 << 20, transcendentals=0),
    )(core, attn, grad, select, unperm)


def feed_back_kernel(chunk, orders, *refs):
    (nt_a, ct_a, nt_b, ct_b, mid_a, gate_a, up_a, mid_b, gate_b, up_b), outs = refs[:10], refs[10:]
    quarter = mid_a.shape[1]
    split = outs[0].shape[1] - quarter
    height = outs[0].shape[0]
    per = height // chunk

    def rows_of(ref, order, place):
        return jnp.concatenate([ref[e * chunk : (e + 1) * chunk, :] for e in order[place * per : (place + 1) * per]], axis=0)

    def total(order, place, left_a, right_a, left_b, right_b):
        return (dot(rows_of(left_a, order, place), right_a) + dot(rows_of(left_b, order, place), right_b)).astype(BF)

    for i in range(2):

        @pl.when(pl.program_id(0) == i)
        def _():
            for side in range(2):
                place = side * 2 + i
                one, two = outs[side], outs[2 + side]
                one[:, :quarter] = total(orders[0], place, nt_a, gate_a[...], nt_b, gate_b[...])
                one[:, quarter:] = total(orders[0], place, ct_a, mid_a[:, :split], ct_b, mid_b[:, :split])
                two[:, :quarter] = total(orders[1], place, nt_a, up_a[...], nt_b, up_b[...])
                two[:, quarter:] = total(orders[1], place, ct_a, mid_a[:, split:], ct_b, mid_b[:, split:])


def feed_back(transposed, acts, chunk, orders, cols):
    width, rows = transposed[0].shape
    quarter = acts[0].shape[1]
    whole = lambda v: pl.BlockSpec(v.shape, lambda i: (0, 0))
    out = lambda c: pl.BlockSpec((width // 4, c), lambda i: (i, 0))
    return pl.pallas_call(
        functools.partial(feed_back_kernel, chunk, orders),
        grid=(2,),
        in_specs=[whole(v) for v in transposed] + [whole(v) for v in acts],
        out_specs=[out(cols[0])] * 2 + [out(cols[1])] * 2,
        out_shape=[jax.ShapeDtypeStruct((width // 2, c), BF) for c in (cols[0], cols[0], cols[1], cols[1])],
        compiler_params=params(),
        cost_estimate=pl.CostEstimate(flops=12 * rows * width * quarter, bytes_accessed=16 << 20, transcendentals=0),
    )(*transposed, *acts)


def down_split(quarter):
    return (quarter // 2 + LANES // 2) // LANES * LANES


def prepare_kernel(
    core_ref, table_ref, q_ref, k_ref, v_ref, o_ref, g_ref, u_ref, d_ref, ga_ref, gm_ref, flags_ref,
    mine_q_ref, theirs_q_ref, mine_f_ref, theirs_f_ref,
):
    first = core_ref[0] == 0
    owned, width = q_ref.shape

    def put(mine_ref, theirs_ref, at, zero, one):
        size = zero.shape[1]
        mine_ref[:, at : at + size] = jnp.where(first, zero, one).astype(BF)
        theirs_ref[:, at : at + size] = jnp.where(first, one, zero).astype(BF)

    for g in range(KV_HEADS):
        at = g * LANES
        kv = slice(g * HEAD, (g + 1) * HEAD)
        zero = jnp.concatenate([q_ref[:, at : at + HEAD], k_ref[:, kv]], axis=1)
        one = jnp.concatenate([q_ref[:, at + HEAD : at + LANES], v_ref[:, kv]], axis=1)
        put(mine_q_ref, theirs_q_ref, at, zero, one)
    shape = (owned, owned)
    diagonal = lax.broadcasted_iota(I32, shape, 0) == lax.broadcasted_iota(I32, shape, 1)
    gain_a = jnp.sum(jnp.where(diagonal, ga_ref[...], 0.0), axis=1, keepdims=True)
    gain_m = jnp.sum(jnp.where(diagonal, gm_ref[...], 0.0), axis=1, keepdims=True)
    count = flags_ref.shape[1]
    cols = count // owned
    row = lax.broadcasted_iota(I32, (owned, count), 0)
    col = lax.broadcasted_iota(I32, (owned, count), 1)
    spread = jnp.where(col // cols == row, flags_ref[...].astype(F32), 0.0).astype(BF)
    row = lax.broadcasted_iota(I32, (count, LANES), 0)
    col = lax.broadcasted_iota(I32, (count, LANES), 1)
    extra = dot(spread, jnp.where(row % cols == col - 3, 1.0, 0.0).astype(BF))
    row = lax.broadcasted_iota(I32, (owned, LANES), 0)
    col = lax.broadcasted_iota(I32, (owned, LANES), 1)
    blocks = jnp.where(row == 0, table_ref[0, 0], jnp.where(row == 1, table_ref[0, 1], 0)).astype(F32)
    extra = jnp.where(col == 0, gain_a, jnp.where(col == 1, gain_m, jnp.where(col == 2, blocks, extra)))
    put(mine_q_ref, theirs_q_ref, width, extra, extra)
    half = g_ref.shape[1] // 2
    quarter = half // 2
    split = down_split(quarter)
    for x in range(2):
        at = 2 * x * quarter * 3 // 2
        for ref, lo, hi in ((g_ref, 0, quarter), (d_ref, 0, split), (u_ref, 0, quarter), (d_ref, split, quarter)):
            zero = ref[:, x * quarter + lo : x * quarter + hi]
            one = ref[:, half + x * quarter + lo : half + x * quarter + hi]
            put(mine_f_ref, theirs_f_ref, at, zero, one)
            at += hi - lo
    put(mine_q_ref, theirs_q_ref, width + LANES, o_ref[:, : width // 2], o_ref[:, width // 2 :])


def prepare(core, table, *arrays):
    owned, width = arrays[0].shape
    cols = 3 * arrays[4].shape[1] // 2
    return pl.pallas_call(
        prepare_kernel,
        in_specs=[in_smem()] * 2 + [in_vmem()] * len(arrays),
        out_specs=[in_vmem()] * 4,
        out_shape=[jax.ShapeDtypeStruct((owned, width + LANES + width // 2), BF)] * 2 + [jax.ShapeDtypeStruct((owned, cols), BF)] * 2,
        compiler_params=params(),
    )(core, table, *arrays)


def deliver_kernel(core_ref, zero_ref, one_ref, other_ref, gate_ref, up_ref, down_ref):
    first = core_ref[0] == 0
    owned, half = gate_ref.shape[0], gate_ref.shape[1] // 2
    quarter = half // 2
    split = down_split(quarter)
    for x, ref in enumerate((zero_ref, one_ref)):
        at = 0
        for out, lo, hi in ((gate_ref, 0, quarter), (down_ref, 0, split), (up_ref, 0, quarter), (down_ref, split, quarter)):
            size = hi - lo
            kept = jnp.where(first, ref[:owned, at : at + size], ref[owned:, at : at + size])
            arrived = other_ref[:, x * 3 * quarter + at : x * 3 * quarter + at + size]
            out[:, x * quarter + lo : x * quarter + hi] = jnp.where(first, kept, arrived)
            out[:, half + x * quarter + lo : half + x * quarter + hi] = jnp.where(first, arrived, kept)
            at += size


def deliver(core, zero, one, other):
    owned, cols = other.shape
    return pl.pallas_call(
        deliver_kernel,
        in_specs=[in_smem()] + [in_vmem()] * 3,
        out_specs=[in_vmem()] * 3,
        out_shape=[jax.ShapeDtypeStruct((owned, 2 * cols // 3), F32)] * 3,
        compiler_params=params(),
    )(core, zero, one, other)


def deliver_heads_kernel(core_ref, qkv_ref, out_ref, other_ref, wo_ref, q_ref, k_ref, v_ref):
    first = core_ref[0] == 0
    owned, width = q_ref.shape
    half = width // 2

    def sides(ref, at, size, shift):
        kept = jnp.where(first, ref[:owned, at : at + size], ref[owned:, at : at + size])
        arrived = other_ref[:, shift + at : shift + at + size]
        return jnp.where(first, kept, arrived), jnp.where(first, arrived, kept)

    wo_ref[:, :half], wo_ref[:, half:] = sides(out_ref, 0, half, width)
    for g in range(0, KV_HEADS, 2):
        zero, one = sides(qkv_ref, g * LANES, LANES, 0)
        zero_next, one_next = sides(qkv_ref, (g + 1) * LANES, LANES, 0)
        q_ref[:, g * LANES : (g + 1) * LANES] = jnp.concatenate([zero[:, :HEAD], one[:, :HEAD]], axis=1)
        q_ref[:, (g + 1) * LANES : (g + 2) * LANES] = jnp.concatenate([zero_next[:, :HEAD], one_next[:, :HEAD]], axis=1)
        k_ref[:, g * HEAD : (g + 2) * HEAD] = jnp.concatenate([zero[:, HEAD:], zero_next[:, HEAD:]], axis=1)
        v_ref[:, g * HEAD : (g + 2) * HEAD] = jnp.concatenate([one[:, HEAD:], one_next[:, HEAD:]], axis=1)


def deliver_heads(core, qkv, out, other):
    owned, width = other.shape[0], qkv.shape[1]
    shapes = [(owned, width), (owned, width), (owned, width // 2), (owned, width // 2)]
    return pl.pallas_call(
        deliver_heads_kernel,
        in_specs=[in_smem()] + [in_vmem()] * 3,
        out_specs=[in_vmem()] * 4,
        out_shape=[jax.ShapeDtypeStruct(e, F32) for e in shapes],
        compiler_params=params(),
    )(core, qkv, out, other)


def leave_kernel(core_ref, own_ref, other_ref, x_ref, wo_ref, gain_ref, res_ref, n_ref, attn_ref, half_ref):
    half = KV_HEADS * HEAD
    for which, ref in enumerate((own_ref, other_ref)):
        for g in range(0, KV_HEADS, 2):
            for s in range(2):
                for j in range(2):
                    lanes = slice(j * HEAD, (j + 1) * HEAD)
                    a = ref[(g * 2 + s) * BLOCK : (g * 2 + s + 1) * BLOCK, lanes]
                    b = ref[((g + 1) * 2 + s) * BLOCK : ((g + 1) * 2 + s + 1) * BLOCK, lanes]
                    row, col = (s * 2 + j) * BLOCK, which * half + g * HEAD
                    attn_ref[row : row + BLOCK, col : col + LANES] = jnp.concatenate([a, b], axis=1)
    value = x_ref[...].astype(F32) + dot(attn_ref[...], wo_ref[...])
    res_ref[...] = value
    inverse = lax.rsqrt(jnp.mean(value * value, axis=-1, keepdims=True) + EPS)
    normed = (value * inverse * gain_ref[...]).astype(BF)
    n_ref[...] = normed
    rows = half_ref.shape[0]
    half_ref[...] = jnp.where(core_ref[0] == 0, normed[:rows], normed[rows:])


def leave(core, own, other, x, wo, gain):
    rows, width = x.shape
    return pl.pallas_call(
        leave_kernel,
        in_specs=[in_smem()] + [in_vmem()] * 5,
        out_specs=[in_vmem()] * 4,
        out_shape=[
            jax.ShapeDtypeStruct((rows, width), F32),
            jax.ShapeDtypeStruct((rows, width), BF),
            jax.ShapeDtypeStruct((rows, width), BF),
            jax.ShapeDtypeStruct((rows // 2, width), BF),
        ],
        compiler_params=params(),
        cost_estimate=pl.CostEstimate(flops=2 * rows * width * width, bytes_accessed=10 << 20, transcendentals=0),
    )(core, own, other, x, wo, gain)


def enter_kernel(
    core_ref, back_ref, other_ref, far_ref, far_other_ref, res_ref, c_ref, gain_ref, wo_ref,
    grad_ref, grad_b_ref, gain_out_ref, out_ref,
):
    value = res_ref[...]
    inverse = lax.rsqrt(jnp.mean(value * value, axis=-1, keepdims=True) + EPS)
    first = core_ref[0] == 0
    far, far_other = far_ref[...].astype(F32), far_other_ref[...].astype(F32)
    far_all = jnp.concatenate([jnp.where(first, far, far_other), jnp.where(first, far_other, far)], axis=0)
    grad = back_ref[...].astype(F32) + other_ref[...].astype(F32) + far_all
    gain_out_ref[...] = jnp.sum(grad * value * inverse, axis=0, keepdims=True)
    scaled = grad * gain_ref[...]
    mean = jnp.mean(scaled * value, axis=-1, keepdims=True)
    total = c_ref[...].astype(F32) + (inverse * scaled - value * (inverse * inverse * inverse) * mean)
    grad_ref[...] = total
    grad_b_ref[...] = total.astype(BF)
    heads = dot(grad_b_ref[...], wo_ref[: KV_HEADS * HEAD, :], NT).astype(BF)
    for g in range(KV_HEADS):
        for s in range(2):
            row = s * 2 * BLOCK
            lanes = slice(g * HEAD, (g + 1) * HEAD)
            out_ref[(g * 2 + s) * BLOCK : (g * 2 + s + 1) * BLOCK, :] = jnp.concatenate(
                [heads[row : row + BLOCK, lanes], heads[row + BLOCK : row + 2 * BLOCK, lanes]], axis=1
            )


def enter(core, back, other, far, far_other, residual, c, gain, wo):
    rows, width = residual.shape
    return pl.pallas_call(
        enter_kernel,
        in_specs=[in_smem()] + [in_vmem()] * 8,
        out_specs=[in_vmem()] * 4,
        out_shape=[
            jax.ShapeDtypeStruct((rows, width), F32),
            jax.ShapeDtypeStruct((rows, width), BF),
            jax.ShapeDtypeStruct((1, width), F32),
            jax.ShapeDtypeStruct((2 * KV_HEADS * BLOCK, LANES), BF),
        ],
        compiler_params=params(),
        cost_estimate=pl.CostEstimate(flops=rows * width * width, bytes_accessed=10 << 20, transcendentals=0),
    )(core, back, other, far, far_other, residual, c, gain, wo)


def rms(value, gain):
    inverse = lax.rsqrt(jnp.mean(value * value, axis=-1, keepdims=True) + EPS)
    return value * inverse * gain, inverse


def rms_back(value, inverse, gain, grad):
    scaled = grad * gain
    mean = jnp.mean(scaled * value, axis=-1, keepdims=True)
    moved = inverse * scaled - value * (inverse * inverse * inverse) * mean
    return moved, jnp.sum(grad * value * inverse, axis=0)


def rope_tables(positions):
    inv_freq = jnp.power(F32(1000000.0), -(2.0 * jnp.arange(HEAD // 2, dtype=F32)) / HEAD)
    angles = positions.astype(F32)[:, None] * inv_freq[None, :]
    cosine, sine = jnp.cos(angles), jnp.sin(angles)
    return (
        jnp.concatenate([cosine] * 4, axis=1),
        jnp.concatenate([-sine, sine, -sine, sine], axis=1),
    )


class Dim:
    def __init__(self, stride, size):
        self.stride, self.size = stride, size


def make_shards(n):
    if n == 16:
        dims = {"x": Dim(1, 2), "y": Dim(2, 2), "p": Dim(4, 2), "q": Dim(8, 2)}
        order_a, order_b, order_m, order_w = "qpxy", "qpyx", "xqpy", "xqyp"
    else:
        names = "abcdefghijkl"[: n.bit_length() - 1]
        dims = {name: Dim(1 << b, 2) for b, name in enumerate(names)}
        order_a = order_b = order_m = order_w = names
    groups = n // 16
    a2a_groups = None if groups == 1 else [[t * 16 + d for d in range(16)] for t in range(groups)]
    kv_groups = None if groups == 1 else [[t * 16 + d for t in range(groups)] for d in range(16)]

    def digits(order):
        places = []
        for r in range(n):
            place = {}
            for name in order:
                place[name] = r % dims[name].size
                r //= dims[name].size
            places.append(place)
        return places

    def place_in(order, base=order_a):
        found = {tuple(sorted(p.items())): r for r, p in enumerate(digits(order))}
        return [found[tuple(sorted(p.items()))] for p in digits(base)]

    def chips(me, order, absolute=None):
        out = []
        for place in digits(order):
            chip = me
            for name, digit in place.items():
                d = dims[name]
                at = (me // d.stride) % d.size
                to = digit if name == absolute else jnp.bitwise_xor(at, digit)
                chip = chip + (to - at) * d.stride
            out.append(chip)
        return jnp.stack(out).astype(I32)

    def ctx_send(value, pairs):
        return lax.ppermute(value, "ctx", pairs)

    def ctx_swap(value, stride):
        return ctx_send(value, [(i, i ^ stride) for i in range(n)])

    def core_swap(value):
        return lax.ppermute(value, "wt", [(0, 1), (1, 0)])

    def gather_dim(value, name):
        return [value, ctx_swap(value, dims[name].stride)]

    def join(parts):
        return parts[0] if len(parts) == 1 else jnp.concatenate(parts, axis=0)

    def gather_rows(parts, names):
        for name in names:
            parts = gather_dim(join(parts), name)
        return parts

    def hold(parts, *others):
        return parts[:-1] + [after(parts[-1], *others)]

    def scatter_begin(keep, send, name):
        return keep, ctx_swap(send.astype(BF), dims[name].stride)

    def scatter_next(state, name):
        keep, arrived = state
        half = keep.shape[0] // 2
        send = (keep[half:].astype(F32) + arrived[half:].astype(F32)).astype(BF)
        return keep[:half].astype(F32) + arrived[:half].astype(F32), ctx_swap(send, dims[name].stride)

    def scatter_end(state):
        keep, arrived = state
        return keep.astype(F32) + arrived.astype(F32)

    def scatter_rows(keep, send, names):
        state = scatter_begin(keep, send, names[-1])
        for name in reversed(names[:-1]):
            state = scatter_next(state, name)
        return scatter_end(state)

    def scatter_whole(value, names):
        half = value.shape[0] // 2
        return scatter_rows(value[:half], value[half:], names)

    def runs(places):
        out = []
        for p in places:
            if out and out[-1][1] == p:
                out[-1][1] = p + 1
            else:
                out.append([p, p + 1])
        return out

    def assemble(parts, order):
        total = sum(p.shape[0] for p in parts)
        unit, each = total // n, parts[0].shape[0] // (total // n)
        out = []
        for lo, hi in runs(place_in(order)):
            while lo < hi:
                part, at = lo // each, lo % each
                stop = min(hi, (part + 1) * each)
                out.append(parts[part][at * unit : (at + stop - lo) * unit])
                lo = stop
        return join(out)

    def columns_in(value, order):
        unit = value.shape[1] // n
        inverse = np.argsort(place_in(order)).tolist()
        pieces = [value[:, lo * unit : hi * unit] for lo, hi in runs(inverse)]
        return pieces[0] if len(pieces) == 1 else jnp.concatenate(pieces, axis=1)

    def after(value, *others):
        return lax.optimization_barrier((value,) + others)[0]

    def swap_heads(value):
        return lax.all_to_all(value, "ctx", 0, 0, axis_index_groups=a2a_groups, tiled=True)

    def shards(
        tokens, block_table, doc_flags, w_query, key_weight, value_weight, w_out, w_gate, w_up, w_down,
        gain_attn, gain_mlp, gain_q, key_norm_gain, cotangent,
    ):
        width = tokens.shape[-1]
        rows = tokens.shape[1]
        owned = w_query.shape[0]
        chip_rows = 2 * owned
        me = lax.axis_index("ctx")
        core = lax.axis_index("wt")
        first = core == 0
        core_arr = core.astype(I32).reshape(1)
        slots_n = 2 * n

        def by_core(a, b, axis=0):
            return jnp.where(first, jnp.concatenate([a, b], axis=axis), jnp.concatenate([b, a], axis=axis))

        def pick(a, b):
            return jnp.where(first, a, b)

        chip_of = chips(me, order_a)

        def features(order, absolute=None):
            chip = chips(me, order, absolute)
            return (chip[:, None] * chip_rows + jnp.arange(chip_rows, dtype=I32)[None, :]).reshape(-1)

        def spread(order, absolute=None):
            return (jnp.arange(width, dtype=I32)[:, None] == features(order, absolute)[None, :]).astype(BF)

        def collect(order, absolute=None):
            return (features(order, absolute)[:, None] == jnp.arange(width, dtype=I32)[None, :]).astype(BF)

        canon = features(order_a)
        perm, perm_m, unperm, unperm_m = lax.optimization_barrier(
            (spread(order_a), spread(order_m, order_m[0]), collect(order_a), collect(order_m, order_m[0]))
        )
        left = me % 2 == 0

        def pick_x(a, b):
            return jnp.where(left, a, b)

        def by_x(a, b, axis=0):
            return pick_x(jnp.concatenate([a, b], axis=axis), jnp.concatenate([b, a], axis=axis))

        flag_cols = rows // owned
        own_blocks = block_table[0]
        mine_q, theirs_q, mine_f, theirs_f = prepare(
            core_arr, block_table, w_query, key_weight, value_weight, w_out, w_gate, w_up, w_down,
            gain_attn[None, :], gain_mlp[None, :], doc_flags,
        )
        first_piece = by_core(mine_q, core_swap(theirs_q))
        acts = jnp.stack([tokens[0], cotangent[0]])
        acts_other = core_swap(acts)
        other_f = core_swap(theirs_f)
        x_two = dot(by_core(acts[0], acts_other[0]), perm).astype(BF)
        x_m = dot(by_core(acts[0], acts_other[0]), perm_m).astype(BF)
        c_m = dot(by_core(acts[1], acts_other[1]), perm_m).astype(BF)
        head_cols = width // 2
        out_cols = width // 4
        out_at = width + LANES

        def cut(value):
            first_cols = [value[:, :head_cols], value[:, width:out_at], value[:, out_at : out_at + out_cols]]
            second_cols = [value[:, head_cols:width], value[:, out_at + out_cols :]]
            return [jnp.concatenate(first_cols, axis=1)], [jnp.concatenate(second_cols, axis=1)]

        if n == 16:
            shared = cut(join(gather_rows([first_piece], "qp")))
            qkv_parts = [gather_rows(shared[0], "x"), gather_rows(shared[1], "y")]
            first_swap = qkv_parts[0][-1]
            qkv_parts = [gather_rows(hold(qkv_parts[0], x_two), "y"), gather_rows(qkv_parts[1], "x")]
        else:
            shared = cut(first_piece)
            qkv_parts = [gather_rows(shared[0], order_a), gather_rows(shared[1], order_b)]
            first_swap = first_piece
        chunk = LANES
        per = chunk // chip_rows
        chunk_orders = [[e // per for e in np.argsort(place_in(o)).tolist()[::per]] for o in (order_a, order_b)]
        extras = assemble([p[:, head_cols : head_cols + LANES] for p in qkv_parts[0]], order_a).astype(F32)
        wo_half = jnp.concatenate(
            [
                assemble([p[:, head_cols + LANES :] for p in qkv_parts[0]], order_a),
                assemble([p[:, head_cols:] for p in qkv_parts[1]], order_b),
            ],
            axis=1,
        )

        hidden = x_two.astype(F32)

        quarter = w_gate.shape[1] // 4
        feed_half = by_core(mine_f, other_f)
        feed_x = feed_half[:, : 3 * quarter], feed_half[:, 3 * quarter :]
        feed_near = pick_x(*feed_x)
        feed_far = after(ctx_swap(pick_x(feed_x[1], feed_x[0]), 1), *shared[0], *shared[1])
        feed_cut = quarter + down_split(quarter)
        feed_cols = (feed_cut, 3 * quarter - feed_cut)
        feed_orders = (order_m[1:], order_w[1:])
        feed_parts = [
            gather_rows([by_x(feed_near[:, lo:hi], feed_far[:, lo:hi])], feed_orders[e][:1])
            for e, (lo, hi) in enumerate(((0, feed_cut), (feed_cut, 3 * quarter)))
        ]

        gain_a, gain_m = extras[:, 0][None, :], extras[:, 1][None, :]
        lane = jnp.arange(BLOCK, dtype=I32)
        n_q = 32 * BLOCK
        own_pos = (own_blocks[:, None] * BLOCK + lane[None, :]).reshape(-1)
        cosine, sine = rope_tables(own_pos)
        gain_qk = jnp.concatenate([gain_q, key_norm_gain])[None, :]

        normed_ab, raw, packed = project(
            core_arr, x_two, gain_a, gain_qk, cosine, sine, qkv_parts, chunk, chunk_orders
        )
        feed_parts = [gather_rows(hold(feed_parts[e], packed), feed_orders[e][1:]) for e in range(2)]
        queries = swap_heads(packed.reshape(16, rows, LANES)).reshape(n_q, LANES)
        own_kv = queries
        gain_mm = dot(dot(jnp.broadcast_to(gain_m, (8, width)).astype(BF), unperm).astype(BF), perm_m)[:1]

        def from_pair(half):
            far = ctx_swap(half, 1)
            return by_core(far, core_swap(far))

        def mine(value):
            return pick(value[:rows], value[rows:])

        def not_mine(value):
            return pick(value[rows:], value[:rows])

        c_far = from_pair(after(mine(c_m), packed))
        if groups > 1:
            own_kv = lax.all_gather(queries, "ctx", axis=0, tiled=True, axis_index_groups=kv_groups)
        other_kv = core_swap(own_kv)
        wo_other = core_swap(wo_half)
        wo_full = by_core(wo_half, wo_other, axis=1)
        head_ids = jnp.arange(width, dtype=I32)
        place = (head_ids // 512).astype(I32)
        head_row = (((head_ids % 512) // HEAD) * 2 + jnp.bitwise_xor(core.astype(I32), place)) * HEAD + head_ids % HEAD
        select = (head_row[:, None] == canon[None, :]).astype(BF)
        wo_sel = dot(select, dot(wo_full, perm_m).astype(BF)).astype(BF)

        extras = after(extras, packed, wo_sel)
        per_chip = extras.reshape(n, 2, owned, LANES)
        block_of = per_chip[:, 0, :2, 2].reshape(-1).astype(I32)
        seq = me % 2
        flags = jnp.where(seq == 0, per_chip[:, 0], per_chip[:, 1])[:, :, 3 : 3 + flag_cols].reshape(slots_n, BLOCK)
        slot_of = (chip_of[:, None] * 2 + jnp.arange(2, dtype=I32)[None, :]).reshape(-1)
        ids = jnp.arange(slots_n, dtype=I32)
        hit = ids[:, None] == block_of[None, :]
        flags_pos = dot(hit.astype(BF), flags.astype(BF))
        kslot = jnp.sum(jnp.where(hit, slot_of[None, :], 0), axis=1)
        pos = jnp.arange(slots_n * BLOCK, dtype=I32).reshape(slots_n, BLOCK)
        begins = jnp.where(flags_pos > 0.5, pos, -1)
        lane = jnp.arange(BLOCK, dtype=I32)
        inside = jnp.max(jnp.where(lane[None, None, :] <= lane[None, :, None], begins[:, None, :], -1), axis=2)
        carried = jnp.max(jnp.where(ids[None, :] < ids[:, None], jnp.max(begins, axis=1)[None, :], -1), axis=1)
        doc_start = jnp.maximum(inside, carried[:, None])
        here = (slot_of // 32) == (me // 16)
        rank = jnp.sum((here[None, :] & (block_of[None, :] < block_of[:, None])).astype(I32), axis=1)
        hit_q = here[None, :] & (rank[None, :] == jnp.arange(32, dtype=I32)[:, None])
        q_block = jnp.sum(jnp.where(hit_q, block_of[None, :], 0), axis=1)
        qslot = jnp.sum(jnp.where(hit_q, slot_of[None, :] - (me // 16) * 32, 0), axis=1)
        q_pos = q_block[:, None] * BLOCK + lane[None, :]
        q_start = jnp.sum(jnp.where((q_block[:, None] == ids[None, :])[:, :, None], doc_start[None], 0), axis=1)
        n_q = 32 * BLOCK
        tile_start = q_start.reshape(n_q // QT, QT)
        tile_pos = q_pos.reshape(n_q // QT, QT)
        low, high = jnp.min(tile_start, axis=1) // KT, jnp.max(tile_pos, axis=1) // KT + 1
        full_low = jnp.minimum((jnp.max(tile_start, axis=1) + KT - 1) // KT, high)
        full_high = jnp.maximum(jnp.minimum((jnp.min(tile_pos, axis=1) + 1) // KT, high), full_low)
        lims = jnp.stack([low, full_low, full_high, high])
        tables = (kslot, qslot, lims, q_pos.reshape(1, n_q), q_start.reshape(1, n_q))

        mixed_packed, mixed, lse = attend(core_arr, tables, queries, own_kv, other_kv)

        attn_own = swap_heads(mixed_packed.reshape(16, BLOCK, LANES)).reshape(16 * BLOCK, LANES)
        residual, normed_m, attn, n_half = leave(core_arr, attn_own, core_swap(attn_own), x_m, wo_sel, gain_mm)

        n_far = from_pair(n_half)
        c_t, c_far_t = turn(c_m, c_far)
        per_chunk = LANES // chip_rows
        feed_chunks = [
            [e // per_chunk for e in np.argsort(place_in(o, order_m)).tolist()[::per_chunk]] for o in (order_m, order_w)
        ]
        *acts_near, out_near, back_near, n_t = feed(normed_m, c_m, feed_parts, LANES, feed_chunks, quarter)
        *acts_far, out_far, back_far, n_far_t = feed(n_far, c_far, feed_parts, LANES, feed_chunks, quarter)
        chip_far = (mine(back_far).astype(F32) + core_swap(not_mine(back_far)).astype(F32)).astype(BF)
        back_pair = ctx_swap(chip_far, 1)
        keep_a, send_a, keep_b, send_b = feed_back(
            (n_t, c_t, n_far_t, c_far_t), (*acts_near, *acts_far), LANES, feed_chunks, feed_cols
        )
        feed_sums = [
            scatter_begin(keep_a, send_a, feed_orders[0][-1]),
            scatter_begin(keep_b, send_b, feed_orders[1][-1]),
        ]
        grad_h, grad_hb, grad_gm, do_packed = enter(
            core_arr, back_near, core_swap(back_near), back_pair, core_swap(back_pair), residual, c_m, gain_mm, wo_sel
        )
        grads_in = swap_heads(do_packed.reshape(16, BLOCK, LANES)).reshape(n_q // 2, LANES)
        attn = after(attn, do_packed)

        out_other = core_swap(jnp.concatenate([not_mine(out_near), not_mine(out_far)]).astype(BF)).astype(F32)
        out_pair = ctx_swap((mine(out_far) + out_other[rows:]).astype(BF), 1).astype(F32)
        layer_rel = mine(residual) + (mine(out_near) + out_other[:rows] + out_pair)
        layer_out = dot(layer_rel.astype(BF), unperm_m).astype(BF)[None]

        grad_wo = out_grad(core_arr, attn, grad_hb, select, unperm_m)
        out_first = grad_wo[:, :out_cols]
        order_rows = np.argsort(place_in(order_b)).tolist()
        out_second = jnp.concatenate(
            [grad_wo[lo * chip_rows : hi * chip_rows, out_cols:] for lo, hi in runs(order_rows)], axis=0
        )

        dq, keep, send = attend_back(core_arr, tables, queries, own_kv, other_kv, grads_in, mixed, lse)
        feed_sums = [scatter_next(hold(list(feed_sums[e]), send), feed_orders[e][-2]) for e in range(2)]
        grad_kv = keep + core_swap(send).astype(F32)
        if groups > 1:
            grad_kv = lax.psum_scatter(grad_kv, "ctx", scatter_dimension=0, tiled=True, axis_index_groups=kv_groups)
        back = swap_heads((dq + grad_kv).astype(BF).reshape(16, rows, LANES))
        grad_qkv_in, gain_parts = unproject(core_arr, back.reshape(KV_HEADS, 2, rows, LANES), raw, gain_qk, cosine, sine)
        g_first, g_second = grad_qkv_in[:, : width // 2], grad_qkv_in[:, width // 2 :]

        def halves(value):
            half = value.shape[0] // 2
            return value[:half], value[half:]

        sum_first = jnp.concatenate([dot(normed_ab, g_first, TN).astype(BF), out_first], axis=1)
        sum_second = jnp.concatenate([dot(columns_in(normed_ab, order_b), g_second, TN).astype(BF), out_second], axis=1)
        level_holds = {}
        if n == 16:
            sum_first = scatter_begin(*halves(sum_first), "y")
            sum_second = scatter_begin(*halves(sum_second), "x")
            level_holds[3] = sum_first[1], sum_second[1]
            sum_first = scatter_next(sum_first, "x")
            sum_second = scatter_next(sum_second, "y")
            level_holds[4] = sum_first[1], sum_second[1]
            sums = jnp.concatenate([scatter_end(sum_first), scatter_end(sum_second)], axis=1)
            sums = scatter_whole(sums, "qp")
        else:
            sums = jnp.concatenate([scatter_whole(sum_first, order_a), scatter_whole(sum_second, order_b)], axis=1)
        cut_cols = head_cols + out_cols
        part_qkv = jnp.concatenate([sums[:, :head_cols], sums[:, cut_cols : cut_cols + head_cols]], axis=1)
        part_out = jnp.concatenate([sums[:, head_cols:cut_cols], sums[:, cut_cols + head_cols :]], axis=1)
        w_first = assemble([p[:, : width // 2] for p in qkv_parts[0]], order_a)
        w_second = assemble([p[:, : width // 2] for p in qkv_parts[1]], order_b)
        n1_part = dot(g_first, w_first, NT) + dot(g_second, w_second, NT)
        n1_other = core_swap(pick(n1_part[rows:], n1_part[:rows]))
        grad_n1 = pick(n1_part[:rows], n1_part[rows:]) + n1_other

        x_mine = mine(hidden)
        _, inv_a = rms(x_mine, gain_a)
        moved_a, grad_ga = rms_back(x_mine, inv_a, gain_a, grad_n1)

        def unspread(value, matrix):
            high = value.astype(BF)
            low = (value - high.astype(F32)).astype(BF)
            return dot(high, matrix) + dot(low, matrix)

        grad_input = (unspread(mine(grad_h), unperm_m) + unspread(moved_a, unperm))[None]

        def exact(vector, matrix):
            return lax.dot_general(
                vector, matrix.astype(F32), NN, precision=lax.Precision.HIGHEST, preferred_element_type=F32
            )

        vectors = jnp.concatenate([exact(grad_ga[None], unperm), exact(jnp.where(first, grad_gm, 0.0), unperm_m)])
        feed_levels = len(order_m)
        for level in range(3, feed_levels):
            feed_sums = [hold(list(v), *level_holds.get(level, ())) for v in feed_sums]
            feed_sums = [scatter_next(feed_sums[e], feed_orders[e][-level]) for e in range(2)]
        feed_sums = [scatter_end(hold(list(v), vectors)) for v in feed_sums]
        feed_near = jnp.concatenate([pick_x(v[:chip_rows], v[chip_rows:]) for v in feed_sums], axis=1)
        feed_far = jnp.concatenate([pick_x(v[chip_rows:], v[:chip_rows]) for v in feed_sums], axis=1)
        feed_far = ctx_swap(feed_far.astype(BF), 1).astype(F32)
        feed_zero, feed_one = pick_x(feed_near, feed_far), pick_x(feed_far, feed_near)
        heads_gain = jnp.sum(gain_parts[:, 0], axis=0)
        chip_gains = jnp.transpose(vectors.reshape(2, n, chip_rows), (1, 0, 2)).reshape(n, 2 * chip_rows)
        small = jnp.concatenate([chip_gains, jnp.broadcast_to(heads_gain[None], (n, LANES))], axis=1)
        small = jnp.pad(small, ((0, 0), (0, 2 * LANES - small.shape[1]))).reshape(n, 1, 2 * LANES)
        small = lax.all_to_all(jnp.broadcast_to(small, (n, 8, 2 * LANES)), "ctx", 0, 0, tiled=True)
        small = jnp.sum(small[:, 0], axis=0)
        small = small + core_swap(small)
        gains = small[: 2 * chip_rows].reshape(2, chip_rows)
        gains = pick(gains[:, :owned], gains[:, owned:])
        head_gains = small[2 * chip_rows : 2 * chip_rows + LANES]

        def theirs(parts):
            return jnp.concatenate([pick(p[owned:], p[:owned]) for p in parts], axis=1)

        grad_gate, grad_up, grad_down = deliver(
            core_arr, feed_zero, feed_one, core_swap(theirs([feed_zero, feed_one]))
        )
        grad_wout, grad_query, grad_key, grad_value = deliver_heads(
            core_arr, part_qkv, part_out, core_swap(theirs([part_qkv, part_out]))
        )
        return (
            layer_out,
            grad_input,
            grad_query,
            grad_key,
            grad_value,
            grad_wout,
            grad_gate,
            grad_up,
            grad_down,
            gains[0],
            gains[1],
            head_gains[:HEAD],
            head_gains[HEAD:],
        )

    return shards


def solution(mesh):
    seq = P("wt", "ctx", None)
    weight = P(("ctx", "wt"), None)
    vector = P(("ctx", "wt"))
    return jax.shard_map(
        make_shards(mesh.shape["ctx"]),
        mesh=mesh,
        in_specs=(seq, P("ctx", None), P("wt", "ctx")) + (weight,) * 7 + (vector, vector, P(), P(), seq),
        out_specs=(seq, seq) + (weight,) * 7 + (vector, vector, P(), P()),
        check_vma=False,
    )
```

profile of v0, /device:TPU:1, one launch (start us, length us, event | category | flops | bytes accessed | tf_op | source)
XLA Modules:
  0.0 487.8 jit_solution(18114872955778216386)
XLA Ops:
  20.6 9.6 %collective-permute-done.1 = bf16[64,1664]{1,0:T(8,128)(2,1)S(1)} collective-permute-done((bf16[64,1664]{1,0:T(8,128)(2,1)S(1)}, bf16[64,1664]{1,0:T(8,128)(2,1)S(1)}, u32[]{:S(2)}, u32[]{:S(2)}) %collective-permute-start.1) | collective-permute-done | bytes 213024 | tf_op jit(solution)/shard_map/ppermute | solution.py:793
  34.1 7.0 %collective-permute-done.2 = bf16[128,1664]{1,0:T(8,128)(2,1)S(1)} collective-permute-done((bf16[128,1664]{1,0:T(8,128)(2,1)S(1)}, bf16[128,1664]{1,0:T(8,128)(2,1)S(1)}, u32[]{:S(2)}, u32[]{:S(2)}) %collective-permute-start.2) | collective-permute-done | bytes 426016 | tf_op jit(solution)/shard_map/ppermute | solution.py:793
  59.6 10.6 %collective-permute-done.7.refs_3_ = bf16[512,768]{1,0:T(8,128)(2,1)S(1)} collective-permute-done((bf16[512,768]{1,0:T(8,128)(2,1)S(1)}, bf16[512,768]{1,0:T(8,128)(2,1)S(1)}, u32[]{:S(2)}, u32[]{:S(2)}) %collective-permute-start.7) | collective-permute-done | bytes 786464 | tf_op jit(solution)/shard_map/ppermute | solution.py:793
  79.8 7.4 %shard_map.247 = (bf16[512,1024]{1,0:T(8,128)(2,1)}, f32[512,1024]{1,0:T(8,128)}, bf16[8,2,256,128]{3,2,1,0:T(8,128)(2,1)}) custom-call(s32[1]{0:T(128)} %bitcast.core_ref, bf16[512,1024]{1,0:T(8,128)(2,1)} %get-tuple-element.203.x_ref, f32[1,1024]{1,0:T(1,128)} %bitcast.167, f32[1,128]{1,0:T(1,128)} %maximum_bitcast_fusion.1.gain_ref, ...), custom_call_target="tpu_custom_call" | custom-call | flops 1073741824 | bytes 8388608 | tf_op jit(solution)/shard_map/pallas_call | solution.py:99
  87.5 9.8 %collective-permute-done.13 = bf16[128,1792]{1,0:T(8,128)(2,1)S(1)} collective-permute-done((bf16[128,1792]{1,0:T(8,128)(2,1)S(1)}, bf16[128,1792]{1,0:T(8,128)(2,1)S(1)}, u32[]{:S(2)}, u32[]{:S(2)}) %collective-permute-start.13) | collective-permute-done | bytes 458784 | tf_op jit(solution)/shard_map/ppermute | solution.py:793
  109.3 8.7 %fusion.36.wo_ref = bf16[1024,1024]{1,0:T(8,128)(2,1)} fusion(s32[1024]{0:T(1024)} %copy-done.87, s32[1024]{0:T(1024)} %copy-done.88, bf16[1024,1024]{1,0:T(8,128)(2,1)} %get-tuple-element.83, bf16[1024,512]{1,0:T(8,128)(2,1)} %collective-permute-done.8, bf16[256,256]{1,0:T(8,128)(2,1)} %copy-done.70, bf16[256,256]{1,0:T(8,128)(2,1)} %copy-done.68, ...), kind=kOutput, calls=%fused_computation.44 | convolution fusion | flops 4328521728 | bytes 6299649 | tf_op jit(solution)/shard_map/dot_general | solution.py:31
  131.0 25.0 %shard_map.248 = (bf16[2048,128]{1,0:T(8,128)(2,1)}, f32[64,4096]{1,0:T(8,128)}, f32[1,4096]{1,0:T(1,128)}) custom-call(s32[1]{0:T(128)} %bitcast.core_ref, s32[32]{0:T(128)} %get-tuple-element.151.kslot_ref, s32[32]{0:T(128)} %get-tuple-element.150.qslot_ref, s32[4,8]{1,0:T(4,128)} %pad_add_fusion.lims_ref, bf16[4096,128]{1,0:T(8,128)(2,1)} %bitcast.47.q_ref.own_ref, ...), custom_call_target="tpu_custom_call" | custom-call | flops 8589934592 | bytes 8388608 | tf_op jit(solution)/shard_map/pallas_call | solution.py:248
  156.0 5.8 %all-to-all-start.1 = ((bf16[16,128,128]{2,1,0:T(8,128)(2,1)}), bf16[16,128,128]{2,1,0:T(8,128)(2,1)}, u32[]{:S(2)}, u32[]{:S(2)}) async-start(bf16[16,128,128]{2,1,0:T(8,128)(2,1)} %bitcast.163), calls=%async_computation.1 | async-start | bytes 1048576 | tf_op jit(solution)/shard_map/all_to_all | solution.py:869
  180.7 5.8 %shard_map.249 = (f32[512,1024]{1,0:T(8,128)}, bf16[512,1024]{1,0:T(8,128)(2,1)}, bf16[512,1024]{1,0:T(8,128)(2,1)}, bf16[256,1024]{1,0:T(8,128)(2,1)}) custom-call(s32[1]{0:T(128)} %bitcast.core_ref, bf16[2048,128]{1,0:T(8,128)(2,1)} %bitcast.51.own_ref, bf16[2048,128]{1,0:T(8,128)(2,1)} %copy-done.67, bf16[512,1024]{1,0:T(8,128)(2,1)} %convolution_convert_fusion.1.x_ref, ...), custom_call_target="tpu_custom_call" | custom-call | flops 1073741824 | bytes 10485760 | tf_op jit(solution)/shard_map/pallas_call | solution.py:669
  187.8 11.5 %collective-permute-done.19 = bf16[256,1024]{1,0:T(8,128)(2,1)S(1)} collective-permute-done((bf16[256,1024]{1,0:T(8,128)(2,1)}, bf16[256,1024]{1,0:T(8,128)(2,1)S(1)}, u32[]{:S(2)}, u32[]{:S(2)}) %collective-permute-start.19) | collective-permute-done | bytes 524320 | tf_op jit(solution)/shard_map/ppermute | solution.py:793
  204.0 6.7 %collective-permute-done.18.refs_3_ = bf16[512,1664]{1,0:T(8,128)(2,1)} collective-permute-done((bf16[512,1664]{1,0:T(8,128)(2,1)}, bf16[512,1664]{1,0:T(8,128)(2,1)}, u32[]{:S(2)}, u32[]{:S(2)}) %collective-permute-start.18) | collective-permute-done | bytes 1703968 | tf_op jit(solution)/shard_map/ppermute | solution.py:793
  215.5 13.4 %shard_map.251 = (bf16[512,1152]{1,0:T(8,128)(2,1)}, bf16[512,1152]{1,0:T(8,128)(2,1)}, bf16[512,1152]{1,0:T(8,128)(2,1)}, f32[512,1024]{1,0:T(8,128)}, bf16[512...) custom-call(bf16[512,1024]{1,0:T(8,128)(2,1)} %maximum_select_fusion.9.n_ref, ...), custom_call_target="tpu_custom_call" | custom-call | flops 7247757312 | bytes 16777216 | tf_op jit(solution)/shard_map/pallas_call | solution.py:435
  234.9 13.5 %shard_map.250 = (bf16[512,1152]{1,0:T(8,128)(2,1)}, bf16[512,1152]{1,0:T(8,128)(2,1)}, bf16[512,1152]{1,0:T(8,128)(2,1)}, f32[512,1024]{1,0:T(8,128)}, bf16[512...) custom-call(bf16[512,1024]{1,0:T(8,128)(2,1)} %get-tuple-element.88.n_ref, bf16[512,1024]{1,0:T(8,128)(2,1)} %copy-done.7, ...), custom_call_target="tpu_custom_call" | custom-call | flops 7247757312 | bytes 16777216 | tf_op jit(solution)/shard_map/pallas_call | solution.py:435
  255.9 6.8 %shard_map.252 = (f32[512,1024]{1,0:T(8,128)}, bf16[512,1024]{1,0:T(8,128)(2,1)}, f32[1,1024]{1,0:T(1,128)}, bf16[2048,128]{1,0:T(8,128)(2,1)}) custom-call(s32[1]{0:T(128)} %bitcast.core_ref, bf16[512,1024]{1,0:T(8,128)(2,1)} %get-tuple-element.99.back_ref, bf16[512,1024]{1,0:T(8,128)(2,1)} %copy-done.60, bf16[256,1024]{1,0:T(8,128)(2,1)} %copy-done.74, ...), custom_call_target="tpu_custom_call" | custom-call | flops 536870912 | bytes 10485760 | tf_op jit(solution)/shard_map/pallas_call | solution.py:712
  262.7 5.5 %all-to-all-start.2 = ((bf16[16,128,128]{2,1,0:T(8,128)(2,1)}), bf16[16,128,128]{2,1,0:T(8,128)(2,1)}, u32[]{:S(2)}, u32[]{:S(2)}) async-start(bf16[16,128,128]{2,1,0:T(8,128)(2,1)} %bitcast.162), calls=%async_computation.2 | async-start | bytes 1048576 | tf_op jit(solution)/shard_map/all_to_all | solution.py:869
  273.7 14.7 %shard_map.258 = (bf16[512,1792]{1,0:T(8,128)(2,1)}, bf16[512,1792]{1,0:T(8,128)(2,1)}, bf16[512,1664]{1,0:T(8,128)(2,1)}, bf16[512,1664]{1,0:T(8,128)(2,1)}) custom-call(bf16[1024,512]{1,0:T(8,128)(2,1)} %get-tuple-element.118.refs_0_, bf16[1024,512]{1,0:T(8,128)(2,1)} %get-tuple-element.119.refs_1_, bf16[1024,512]{1,0:T(8,128)(2,1)} %get-tuple-element.120.refs_2_, ...), custom_call_target="tpu_custom_call" | custom-call | flops 7247757312 | bytes 16777216 | tf_op jit(solution)/shard_map/pallas_call | solution.py:513
  296.1 39.8 %shard_map.253 = (f32[4096,128]{1,0:T(8,128)}, f32[4096,128]{1,0:T(8,128)}, bf16[4096,128]{1,0:T(8,128)(2,1)}) custom-call(s32[1]{0:T(128)} %bitcast.core_ref, s32[32]{0:T(128)} %get-tuple-element.151.kslot_ref, s32[32]{0:T(128)} %get-tuple-element.150.qslot_ref, s32[4,8]{1,0:T(4,128)} %pad_add_fusion.lims_ref, bf16[4096,128]{1,0:T(8,128)(2,1)} %bitcast.47.q_ref.own_ref, ...), custom_call_target="tpu_custom_call" | custom-call | flops 17179869184 | bytes 8388608 | tf_op jit(solution)/shard_map/pallas_call | solution.py:358
  342.3 6.4 %shard_map.255 = bf16[1024,512]{1,0:T(8,128)(2,1)} custom-call(s32[1]{0:T(128)} %bitcast.core_ref, bf16[512,1024]{1,0:T(8,128)(2,1)} %get-tuple-element.112.attn_ref, bf16[512,1024]{1,0:T(8,128)(2,1)} %get-tuple-element.113.grad_ref, bf16[1024,1024]{1,0:T(8,128)(2,1)} %get-tuple-element.181.select_ref, bf16[1024,1024]{1,0:T(8,128)(2,1)} %get-tuple-element.98.unperm_ref), custom_call_target="tpu_custom_call" | custom-call | flops 4294967296 | bytes 8388608 | tf_op jit(solution)/shard_map/pallas_call | solution.py:472
  373.8 5.3 %all-to-all-done.3 = bf16[16,256,128]{2,1,0:T(8,128)(2,1)} async-done(((bf16[16,256,128]{2,1,0:T(8,128)(2,1)}), bf16[16,256,128]{2,1,0:T(8,128)(2,1)}, u32[]{:S(2)}, u32[]{:S(2)}) %all-to-all-start.3) | async-done | bytes 1048608 | tf_op jit(solution)/shard_map/all_to_all | solution.py:869
  379.1 8.3 %shard_map.254 = (bf16[512,1024]{1,0:T(8,128)(2,1)}, f32[8,8,128]{2,1,0:T(8,128)}) custom-call(s32[1]{0:T(128)} %bitcast.core_ref, bf16[8,2,256,128]{3,2,1,0:T(8,128)(2,1)} %bitcast.58.grad_ref, f32[512,1024]{1,0:T(8,128)} %get-tuple-element.108.raw_ref, f32[1,128]{1,0:T(1,128)} %maximum_bitcast_fusion.1.gain_ref, f32[256,128]{1,0:T(8,128)} %pad_maximum_fusion.24.cos_ref, ...), custom_call_target="tpu_custom_call" | custom-call | flops 16777216 | bytes 8388608 | tf_op jit(solution)/shard_map/pallas_call | solution.py:138
  398.6 9.7 %collective-permute-done.31 = bf16[512,768]{1,0:T(8,128)(2,1)S(1)} collective-permute-done((bf16[512,768]{1,0:T(8,128)(2,1)S(1)}, bf16[512,768]{1,0:T(8,128)(2,1)S(1)}, u32[]{:S(2)}, u32[]{:S(2)}) %collective-permute-start.31) | collective-permute-done | bytes 786464 | tf_op jit(solution)/shard_map/ppermute | solution.py:793
  422.5 5.4 %all-to-all-start.4 = ((f32[16,8,256]{2,1,0:T(8,128)}), f32[16,8,256]{2,1,0:T(8,128)S(1)}, u32[]{:S(2)}, u32[]{:S(2)}) async-start(f32[16,8,256]{2,1,0:T(8,128)} %broadcast_in_dim.174), calls=%async_computation.4 | async-start | bytes 262144 | tf_op jit(solution)/shard_map/all_to_all | solution.py:1148
  437.2 9.0 %collective-permute-done.43 = bf16[128,1664]{1,0:T(8,128)(2,1)} collective-permute-done((bf16[128,1664]{1,0:T(8,128)(2,1)}, bf16[128,1664]{1,0:T(8,128)(2,1)}, u32[]{:S(2)}, u32[]{:S(2)}) %collective-permute-start.43) | collective-permute-done | bytes 426016 | tf_op jit(solution)/shard_map/ppermute | solution.py:793
  447.6 8.5 %collective-permute-done.40 = bf16[128,1792]{1,0:T(8,128)(2,1)} collective-permute-done((bf16[128,1792]{1,0:T(8,128)(2,1)}, bf16[128,1792]{1,0:T(8,128)(2,1)}, u32[]{:S(2)}, u32[]{:S(2)}) %collective-permute-start.40) | collective-permute-done | bytes 458784 | tf_op jit(solution)/shard_map/ppermute | solution.py:793
  (460 shorter events, 231.5 us)
Async XLA Ops:
  2.9 40.6 %collective-permute-start.4 = (bf16[2,256,1024]{2,1,0:T(8,128)(2,1)}, bf16[2,256,1024]{2,1,0:T(8,128)(2,1)S(1)}, u32[]{:S(2)}, u32[]{:S(2)}) collective-permute-start(bf16[2,256,1024]{2,1,0:T(8,128)(2,1)} %pad_maximum_fusion.2), channel_id=1, source_target_pairs={{0,1},{1,0},{2,3},{3,2},{4,5},{5,4},{6,7},{7,6},{8,9},{9,8},{10,11... | collective-permute-start | bytes 3145736 | tf_op jit(solution)/shard_map/ppermute | solution.py:799
  6.2 24.8 %collective-permute-start.11 = (bf16[32,6912]{1,0:T(8,128)(2,1)}, bf16[32,6912]{1,0:T(8,128)(2,1)}, u32[]{:S(2)}, u32[]{:S(2)}) collective-permute-start(bf16[32,6912]{1,0:T(8,128)(2,1)} %get-tuple-element.90), channel_id=1, source_target_pairs={{0,1},{1,0},{2,3},{3,2},{4,5},{5,4},{6,7},{7,6},{8,9},{9,8},{10,11... | collective-permute-start | bytes 1327112 | tf_op jit(solution)/shard_map/ppermute | solution.py:799
  55.4 32.1 %collective-permute-start.16 = (bf16[128,1664]{1,0:T(8,128)(2,1)S(1)}, bf16[128,1664]{1,0:T(8,128)(2,1)S(1)}, u32[]{:S(2)}, u32[]{:S(2)}) collective-permute-start(bf16[128,1664]{1,0:T(8,128)(2,1)S(1)} %maximum_select_fusion.13), channel_id=1, source_target_pairs={{0,16},{2,18},{4,20},{6,22},{8,24},{10,26},{12,28},{14,30},{16,0},... | collective-permute-start | bytes 1277960 | tf_op jit(solution)/shard_map/ppermute | solution.py:793
  59.4 37.9 %collective-permute-start.13 = (bf16[128,1792]{1,0:T(8,128)(2,1)S(1)}, bf16[128,1792]{1,0:T(8,128)(2,1)S(1)}, u32[]{:S(2)}, u32[]{:S(2)}) collective-permute-start(bf16[128,1792]{1,0:T(8,128)(2,1)S(1)} %maximum_select_fusion.12), channel_id=1, source_target_pairs={{0,16},{2,18},{4,20},{6,22},{8,24},{10,26},{12,28},{14,30},{16,0},... | collective-permute-start | bytes 1376264 | tf_op jit(solution)/shard_map/ppermute | solution.py:793
  72.5 36.8 %collective-permute-start.8 = (bf16[1024,512]{1,0:T(8,128)(2,1)}, bf16[1024,512]{1,0:T(8,128)(2,1)}, u32[]{:S(2)}, u32[]{:S(2)}) collective-permute-start(bf16[1024,512]{1,0:T(8,128)(2,1)} %maximum_maximum_fusion.1), channel_id=1, source_target_pairs={{0,1},{1,0},{2,3},{3,2},{4,5},{5,4},{6,7},{7,6},{8,9},{9,8},{10,11... | collective-permute-start | bytes 3145736 | tf_op jit(solution)/shard_map/ppermute | solution.py:799
  98.1 27.7 %all-to-all-start = ((bf16[16,256,128]{2,1,0:T(8,128)(2,1)}), bf16[16,256,128]{2,1,0:T(8,128)(2,1)}, u32[]{:S(2)}, u32[]{:S(2)}) async-start(bf16[16,256,128]{2,1,0:T(8,128)(2,1)} %bitcast.161), calls=%async_computation | async-start | bytes 2097152 | tf_op jit(solution)/shard_map/all_to_all | solution.py:869
  104.7 64.2 %collective-permute-start.17 = (bf16[256,1664]{1,0:T(8,128)(2,1)}, bf16[256,1664]{1,0:T(8,128)(2,1)}, u32[]{:S(2)}, u32[]{:S(2)}) collective-permute-start(bf16[256,1664]{1,0:T(8,128)(2,1)} %pad_maximum_fusion.9), channel_id=1, source_target_pairs={{0,4},{2,6},{4,0},{6,2},{8,12},{10,14},{12,8},{14,10},{16,20},{18,... | collective-permute-start | bytes 2555912 | tf_op jit(solution)/shard_map/ppermute | solution.py:793
  108.1 64.6 %collective-permute-start.14 = (bf16[256,1792]{1,0:T(8,128)(2,1)}, bf16[256,1792]{1,0:T(8,128)(2,1)}, u32[]{:S(2)}, u32[]{:S(2)}) collective-permute-start(bf16[256,1792]{1,0:T(8,128)(2,1)} %pad_maximum_fusion.5), channel_id=1, source_target_pairs={{0,8},{2,10},{4,12},{6,14},{8,0},{10,2},{12,4},{14,6},{16,24},{18,... | collective-permute-start | bytes 2752520 | tf_op jit(solution)/shard_map/ppermute | solution.py:793
  171.4 39.2 %collective-permute-start.18 = (bf16[512,1664]{1,0:T(8,128)(2,1)}, bf16[512,1664]{1,0:T(8,128)(2,1)}, u32[]{:S(2)}, u32[]{:S(2)}) collective-permute-start(bf16[512,1664]{1,0:T(8,128)(2,1)} %pad_maximum_fusion.1.refs_2_), channel_id=1, source_target_pairs={{0,8},{2,10},{4,12},{6,14},{8,0},{10,2},{12,4},{14,6},{16,24},{18,... | collective-permute-start | bytes 5111816 | tf_op jit(solution)/shard_map/ppermute | solution.py:793
  175.2 40.3 %collective-permute-start.15 = (bf16[512,1792]{1,0:T(8,128)(2,1)}, bf16[512,1792]{1,0:T(8,128)(2,1)}, u32[]{:S(2)}, u32[]{:S(2)}) collective-permute-start(bf16[512,1792]{1,0:T(8,128)(2,1)} %pad_maximum_fusion.refs_0_), channel_id=1, source_target_pairs={{0,4},{2,6},{4,0},{6,2},{8,12},{10,14},{12,8},{14,10},{16,20},{18,... | collective-permute-start | bytes 5505032 | tf_op jit(solution)/shard_map/ppermute | solution.py:793
  253.4 37.6 %collective-permute-start.23 = (bf16[512,1024]{1,0:T(8,128)(2,1)}, bf16[512,1024]{1,0:T(8,128)(2,1)}, u32[]{:S(2)}, u32[]{:S(2)}) collective-permute-start(bf16[512,1024]{1,0:T(8,128)(2,1)} %pad_maximum_fusion.3), channel_id=1, source_target_pairs={{0,1},{1,0},{2,3},{3,2},{4,5},{5,4},{6,7},{7,6},{8,9},{9,8},{10,11... | collective-permute-start | bytes 3145736 | tf_op jit(solution)/shard_map/ppermute | solution.py:799
  262.7 33.4 %all-to-all-start.2 = ((bf16[16,128,128]{2,1,0:T(8,128)(2,1)}), bf16[16,128,128]{2,1,0:T(8,128)(2,1)}, u32[]{:S(2)}, u32[]{:S(2)}) async-start(bf16[16,128,128]{2,1,0:T(8,128)(2,1)} %bitcast.162), calls=%async_computation.2 | async-start | bytes 1048576 | tf_op jit(solution)/shard_map/all_to_all | solution.py:869
  288.3 76.3 %collective-permute-start.41 = (bf16[512,1664]{1,0:T(8,128)(2,1)}, bf16[512,1664]{1,0:T(8,128)(2,1)}, u32[]{:S(2)}, u32[]{:S(2)}) collective-permute-start(bf16[512,1664]{1,0:T(8,128)(2,1)} %get-tuple-element.135), channel_id=1, source_target_pairs={{0,8},{2,10},{4,12},{6,14},{8,0},{10,2},{12,4},{14,6},{16,24},{18,... | collective-permute-start | bytes 5111816 | tf_op jit(solution)/shard_map/ppermute | solution.py:793
  289.9 79.3 %collective-permute-start.38 = (bf16[512,1792]{1,0:T(8,128)(2,1)}, bf16[512,1792]{1,0:T(8,128)(2,1)}, u32[]{:S(2)}, u32[]{:S(2)}) collective-permute-start(bf16[512,1792]{1,0:T(8,128)(2,1)} %get-tuple-element.129), channel_id=1, source_target_pairs={{0,4},{2,6},{4,0},{6,2},{8,12},{10,14},{12,8},{14,10},{16,20},{18,... | collective-permute-start | bytes 5505032 | tf_op jit(solution)/shard_map/ppermute | solution.py:793
  294.9 42.4 %collective-permute-start.24 = (bf16[256,1024]{1,0:T(8,128)(2,1)}, bf16[256,1024]{1,0:T(8,128)(2,1)}, u32[]{:S(2)}, u32[]{:S(2)}) collective-permute-start(bf16[256,1024]{1,0:T(8,128)(2,1)} %fusion.45), channel_id=1, source_target_pairs={{0,2},{2,0},{4,6},{6,4},{8,10},{10,8},{12,14},{14,12},{16,18},{18,... | collective-permute-start | bytes 1572872 | tf_op jit(solution)/shard_map/ppermute | solution.py:793
  351.2 27.9 %all-to-all-start.3 = ((bf16[16,256,128]{2,1,0:T(8,128)(2,1)}), bf16[16,256,128]{2,1,0:T(8,128)(2,1)}, u32[]{:S(2)}, u32[]{:S(2)}) async-start(bf16[16,256,128]{2,1,0:T(8,128)(2,1)} %bitcast.158), calls=%async_computation.3 | async-start | bytes 2097152 | tf_op jit(solution)/shard_map/all_to_all | solution.py:869
  368.0 44.2 %collective-permute-start.42 = (bf16[256,1664]{1,0:T(8,128)(2,1)}, bf16[256,1664]{1,0:T(8,128)(2,1)}, u32[]{:S(2)}, u32[]{:S(2)}) collective-permute-start(bf16[256,1664]{1,0:T(8,128)(2,1)} %get-tuple-element.157), channel_id=1, source_target_pairs={{0,4},{2,6},{4,0},{6,2},{8,12},{10,14},{12,8},{14,10},{16,20},{18,... | collective-permute-start | bytes 2555912 | tf_op jit(solution)/shard_map/ppermute | solution.py:793
  372.6 44.9 %collective-permute-start.39 = (bf16[256,1792]{1,0:T(8,128)(2,1)}, bf16[256,1792]{1,0:T(8,128)(2,1)}, u32[]{:S(2)}, u32[]{:S(2)}) collective-permute-start(bf16[256,1792]{1,0:T(8,128)(2,1)} %get-tuple-element.155), channel_id=1, source_target_pairs={{0,8},{2,10},{4,12},{6,14},{8,0},{10,2},{12,4},{14,6},{16,24},{18,... | collective-permute-start | bytes 2752520 | tf_op jit(solution)/shard_map/ppermute | solution.py:793
  396.2 23.2 %collective-permute-start.30 = (f32[256,1024]{1,0:T(8,128)S(1)}, f32[256,1024]{1,0:T(8,128)S(1)}, u32[]{:S(2)}, u32[]{:S(2)}) collective-permute-start(f32[256,1024]{1,0:T(8,128)S(1)} %slice_select_fusion.2), channel_id=1, source_target_pairs={{0,1},{1,0},{2,3},{3,2},{4,5},{5,4},{6,7},{7,6},{8,9},{9,8},{10,11... | collective-permute-start | bytes 3145736 | tf_op jit(solution)/shard_map/ppermute | solution.py:799
  409.2 22.8 %collective-permute-start.32 = (bf16[256,768]{1,0:T(8,128)(2,1)}, bf16[256,768]{1,0:T(8,128)(2,1)}, u32[]{:S(2)}, u32[]{:S(2)}) collective-permute-start(bf16[256,768]{1,0:T(8,128)(2,1)} %add_convert_fusion.5), channel_id=1, source_target_pairs={{0,2},{2,0},{4,6},{6,4},{8,10},{10,8},{12,14},{14,12},{16,18},{18,... | collective-permute-start | bytes 1179656 | tf_op jit(solution)/shard_map/ppermute | solution.py:793
  414.0 32.2 %collective-permute-start.43 = (bf16[128,1664]{1,0:T(8,128)(2,1)}, bf16[128,1664]{1,0:T(8,128)(2,1)}, u32[]{:S(2)}, u32[]{:S(2)}) collective-permute-start(bf16[128,1664]{1,0:T(8,128)(2,1)} %fusion.75), channel_id=1, source_target_pairs={{0,16},{2,18},{4,20},{6,22},{8,24},{10,26},{12,28},{14,30},{16,0},... | collective-permute-start | bytes 1277960 | tf_op jit(solution)/shard_map/ppermute | solution.py:793
  419.3 36.7 %collective-permute-start.40 = (bf16[128,1792]{1,0:T(8,128)(2,1)}, bf16[128,1792]{1,0:T(8,128)(2,1)}, u32[]{:S(2)}, u32[]{:S(2)}) collective-permute-start(bf16[128,1792]{1,0:T(8,128)(2,1)} %fusion.73), channel_id=1, source_target_pairs={{0,16},{2,18},{4,20},{6,22},{8,24},{10,26},{12,28},{14,30},{16,0},... | collective-permute-start | bytes 1376264 | tf_op jit(solution)/shard_map/ppermute | solution.py:793
  422.5 35.3 %all-to-all-start.4 = ((f32[16,8,256]{2,1,0:T(8,128)}), f32[16,8,256]{2,1,0:T(8,128)S(1)}, u32[]{:S(2)}, u32[]{:S(2)}) async-start(f32[16,8,256]{2,1,0:T(8,128)} %broadcast_in_dim.174), calls=%async_computation.4 | async-start | bytes 262144 | tf_op jit(solution)/shard_map/all_to_all | solution.py:1148
  435.8 27.8 %collective-permute-start.35 = (bf16[128,1536]{1,0:T(8,128)(2,1)}, bf16[128,1536]{1,0:T(8,128)(2,1)}, u32[]{:S(2)}, u32[]{:S(2)}) collective-permute-start(bf16[128,1536]{1,0:T(8,128)(2,1)} %fusion.79), channel_id=1, source_target_pairs={{0,8},{2,10},{4,12},{6,14},{8,0},{10,2},{12,4},{14,6},{16,24},{18,... | collective-permute-start | bytes 1179656 | tf_op jit(solution)/shard_map/ppermute | solution.py:793
  (126 other events, 1086.8 us)
where the time goes:
time: 487 us; the launch traced here: 488 us
  Pallas kernels  152 us (31%)
  waiting for transfers between devices  108 us (22%)
  starting transfers between devices  92.9 us (19%)
  other arithmetic  70.9 us (15%)
  matrix products  38.6 us (8%)
  local copies, waits for them, and re-layouts  23.1 us (5%)
    ppermute x30, waiting for transfers between devices, ctx_send(): return lax.ppermute(value, 'ctx', pairs)  101 us
    ppermute x30, starting transfers between devices, ctx_send(): return lax.ppermute(value, 'ctx', pairs)  42.2 us
    pallas_call x1, Pallas kernels, attend_back(): pl.pallas_call(attend_back_kernel, in_specs=[in_smem()] * 4 + [in_vmem()]...  39.8 us
    dot_general x16, matrix products, dot(): return lax.dot_general(a, b, dims, preferred_element_type=F32)  36.7 us
    pallas_call x2, Pallas kernels, feed(): pl.pallas_call(functools.partial(feed_kernel, len(parts[0]), chunk, order...  26.8 us
    ppermute x17, starting transfers between devices, core_swap(): return lax.ppermute(value, 'wt', [(0, 1), (1, 0)])  25 us
    pallas_call x1, Pallas kernels, attend(): pl.pallas_call(attend_kernel, in_specs=[in_smem()] * 4 + [in_vmem()] * 5,...  25 us
    all_to_all x4, starting transfers between devices, swap_heads(): lax.all_to_all(value, 'ctx', 0, 0, axis_index_groups=a2a_groups, tiled=True)  20.2 us
  transfers between devices with their start and end apart: 52, of which 23 were waited for; matrix products, arithmetic and copies ran while one was open for 25% of the time, Pallas kernels for 28%

commit v1 on v0

--- a/solution.py
+++ b/solution.py
@@ -819,7 +819,8 @@
         keep, arrived = state
         half = keep.shape[0] // 2
         send = (keep[half:].astype(F32) + arrived[half:].astype(F32)).astype(BF)
-        return keep[:half].astype(F32) + arrived[:half].astype(F32), ctx_swap(send, dims[name].stride)
+        keep = (keep[:half].astype(F32) + arrived[:half].astype(F32)).astype(BF)
+        return keep, ctx_swap(send, dims[name].stride)
 
     def scatter_end(state):
         keep, arrived = state
@@ -890,20 +891,16 @@
 
         chip_of = chips(me, order_a)
 
-        def features(order, absolute=None):
+        def features(order, me, absolute=None):
             chip = chips(me, order, absolute)
             return (chip[:, None] * chip_rows + jnp.arange(chip_rows, dtype=I32)[None, :]).reshape(-1)
 
-        def spread(order, absolute=None):
-            return (jnp.arange(width, dtype=I32)[:, None] == features(order, absolute)[None, :]).astype(BF)
-
-        def collect(order, absolute=None):
-            return (features(order, absolute)[:, None] == jnp.arange(width, dtype=I32)[None, :]).astype(BF)
-
-        canon = features(order_a)
-        perm, perm_m, unperm, unperm_m = lax.optimization_barrier(
-            (spread(order_a), spread(order_m, order_m[0]), collect(order_a), collect(order_m, order_m[0]))
-        )
+        def spread(order, me, absolute=None):
+            return (jnp.arange(width, dtype=I32)[:, None] == features(order, me, absolute)[None, :]).astype(BF)
+
+        def collect(order, me, absolute=None):
+            return (features(order, me, absolute)[:, None] == jnp.arange(width, dtype=I32)[None, :]).astype(BF)
+
         left = me % 2 == 0
 
         def pick_x(a, b):
@@ -919,13 +916,23 @@
             gain_attn[None, :], gain_mlp[None, :], doc_flags,
         )
         first_piece = by_core(mine_q, core_swap(theirs_q))
-        acts = jnp.stack([tokens[0], cotangent[0]])
+        acts = jnp.stack([after(tokens[0], mine_q), after(cotangent[0], mine_q)])
         acts_other = core_swap(acts)
         other_f = core_swap(theirs_f)
+        me_later = after(me.astype(I32), first_piece)
+        canon = features(order_a, me_later)
+        perm, perm_m, unperm, unperm_m = lax.optimization_barrier(
+            (spread(order_a, me_later), spread(order_m, me_later, order_m[0]), collect(order_a, me_later), collect(order_m, me_later, order_m[0]))
+        )
         x_two = dot(by_core(acts[0], acts_other[0]), perm).astype(BF)
         x_m = dot(by_core(acts[0], acts_other[0]), perm_m).astype(BF)
         c_m = dot(by_core(acts[1], acts_other[1]), perm_m).astype(BF)
         head_cols = width // 2
+        quarter = w_gate.shape[1] // 4
+        feed_half = by_core(mine_f, other_f)
+        feed_x = feed_half[:, : 3 * quarter], feed_half[:, 3 * quarter :]
+        feed_near = pick_x(*feed_x)
+        feed_far = ctx_swap(pick_x(feed_x[1], feed_x[0]), 1)
         out_cols = width // 4
         out_at = width + LANES
 
@@ -935,7 +942,9 @@
             return [jnp.concatenate(first_cols, axis=1)], [jnp.concatenate(second_cols, axis=1)]
 
         if n == 16:
-            shared = cut(join(gather_rows([first_piece], "qp")))
+            halfway = hold(gather_rows([first_piece], "q"), feed_far)
+            feed_far = after(feed_far, halfway[-1])
+            shared = cut(join(gather_rows(halfway, "p")))
             qkv_parts = [gather_rows(shared[0], "x"), gather_rows(shared[1], "y")]
             first_swap = qkv_parts[0][-1]
             qkv_parts = [gather_rows(hold(qkv_parts[0], x_two), "y"), gather_rows(qkv_parts[1], "x")]
@@ -957,11 +966,6 @@
 
         hidden = x_two.astype(F32)
 
-        quarter = w_gate.shape[1] // 4
-        feed_half = by_core(mine_f, other_f)
-        feed_x = feed_half[:, : 3 * quarter], feed_half[:, 3 * quarter :]
-        feed_near = pick_x(*feed_x)
-        feed_far = after(ctx_swap(pick_x(feed_x[1], feed_x[0]), 1), *shared[0], *shared[1])
         feed_cut = quarter + down_split(quarter)
         feed_cols = (feed_cut, 3 * quarter - feed_cut)
         feed_orders = (order_m[1:], order_w[1:])
@@ -987,7 +991,7 @@
 
         def from_pair(half):
             far = ctx_swap(half, 1)
-            return by_core(far, core_swap(far))
+            return jnp.concatenate([far, core_swap(far)])
 
         def mine(value):
             return pick(value[:rows], value[rows:])
@@ -1051,8 +1055,8 @@
             [e // per_chunk for e in np.argsort(place_in(o, order_m)).tolist()[::per_chunk]] for o in (order_m, order_w)
         ]
         *acts_near, out_near, back_near, n_t = feed(normed_m, c_m, feed_parts, LANES, feed_chunks, quarter)
-        *acts_far, out_far, back_far, n_far_t = feed(n_far, c_far, feed_parts, LANES, feed_chunks, quarter)
-        chip_far = (mine(back_far).astype(F32) + core_swap(not_mine(back_far)).astype(F32)).astype(BF)
+        *acts_far, out_far, back_far, n_far_t = feed(after(n_far, c_t, c_far_t), c_far, feed_parts, LANES, feed_chunks, quarter)
+        chip_far = (back_far[:rows].astype(F32) + core_swap(back_far[rows:]).astype(F32)).astype(BF)
         back_pair = ctx_swap(chip_far, 1)
         keep_a, send_a, keep_b, send_b = feed_back(
             (n_t, c_t, n_far_t, c_far_t), (*acts_near, *acts_far), LANES, feed_chunks, feed_cols
@@ -1067,8 +1071,8 @@
         grads_in = swap_heads(do_packed.reshape(16, BLOCK, LANES)).reshape(n_q // 2, LANES)
         attn = after(attn, do_packed)
 
-        out_other = core_swap(jnp.concatenate([not_mine(out_near), not_mine(out_far)]).astype(BF)).astype(F32)
-        out_pair = ctx_swap((mine(out_far) + out_other[rows:]).astype(BF), 1).astype(F32)
+        out_other = core_swap(jnp.concatenate([not_mine(out_near), out_far[rows:]]).astype(BF)).astype(F32)
+        out_pair = ctx_swap((out_far[:rows] + out_other[rows:]).astype(BF), 1).astype(F32)
         layer_rel = mine(residual) + (mine(out_near) + out_other[:rows] + out_pair)
         layer_out = dot(layer_rel.astype(BF), unperm_m).astype(BF)[None]
 
@@ -1079,12 +1083,14 @@
             [grad_wo[lo * chip_rows : hi * chip_rows, out_cols:] for lo, hi in runs(order_rows)], axis=0
         )
 
+        grads_in = after(grads_in, send_a, send_b)
         dq, keep, send = attend_back(core_arr, tables, queries, own_kv, other_kv, grads_in, mixed, lse)
         feed_sums = [scatter_next(hold(list(feed_sums[e]), send), feed_orders[e][-2]) for e in range(2)]
         grad_kv = keep + core_swap(send).astype(F32)
         if groups > 1:
             grad_kv = lax.psum_scatter(grad_kv, "ctx", scatter_dimension=0, tiled=True, axis_index_groups=kv_groups)
-        back = swap_heads((dq + grad_kv).astype(BF).reshape(16, rows, LANES))
+        payload = (dq + grad_kv).astype(BF)
+        back = swap_heads(payload.reshape(16, rows, LANES))
         grad_qkv_in, gain_parts = unproject(core_arr, back.reshape(KV_HEADS, 2, rows, LANES), raw, gain_qk, cosine, sine)
         g_first, g_second = grad_qkv_in[:, : width // 2], grad_qkv_in[:, width // 2 :]
 

time: 487 us -> 478 us (0.982); the launches traced: 488 us -> 472 us
  other arithmetic: 70.9 us -> 61.6 us
  Pallas kernels: 152 us -> 145 us
  local copies, waits for them, and re-layouts: 23.1 us -> 29.9 us
  waiting for transfers between devices: 108 us -> 102 us
    ppermute x30, waiting for transfers between devices: 101 us -> 91.3 us  [ctx_send(): return lax.ppermute(value, 'ctx', pairs)]
    select_n x4 -> x2, other arithmetic: 5.7 us -> 0.18 us  [by_core(): jnp.where(first, jnp.concatenate([a, b], axis=axis), jnp.concatenate([b,...]
    unnamed x193 -> x200, local copies, waits for them, and re-layouts: 8.41 us -> 10.8 us
  transfers between devices with their start and end apart: 52 -> 52, of which waited for: 23 -> 20; matrix products, arithmetic and copies ran while one was open for 25% -> 25% of each run, Pallas kernels for 28% -> 27%
where the time goes in v1:
time: 478 us; the launch traced here: 472 us
  Pallas kernels  145 us (30%)
  waiting for transfers between devices  102 us (21%)
  starting transfers between devices  92.5 us (19%)
  other arithmetic  61.6 us (13%)
  matrix products  38.6 us (8%)
  local copies, waits for them, and re-layouts  29.9 us (6%)
    ppermute x30, waiting for transfers between devices, ctx_send(): return lax.ppermute(value, 'ctx', pairs)  91.3 us
    ppermute x30, starting transfers between devices, ctx_send(): return lax.ppermute(value, 'ctx', pairs)  39.5 us
    dot_general x16, matrix products, dot(): return lax.dot_general(a, b, dims, preferred_element_type=F32)  36.7 us
    pallas_call x1, Pallas kernels, attend_back(): pl.pallas_call(attend_back_kernel, in_specs=[in_smem()] * 4 + [in_vmem()]...  35.4 us
    pallas_call x2, Pallas kernels, feed(): pl.pallas_call(functools.partial(feed_kernel, len(parts[0]), chunk, order...  27 us
    ppermute x17, starting transfers between devices, core_swap(): return lax.ppermute(value, 'wt', [(0, 1), (1, 0)])  26.5 us
    pallas_call x1, Pallas kernels, attend(): pl.pallas_call(attend_kernel, in_specs=[in_smem()] * 4 + [in_vmem()] * 5,...  22.3 us
    all_to_all x4, starting transfers between devices, swap_heads(): lax.all_to_all(value, 'ctx', 0, 0, axis_index_groups=a2a_groups, tiled=True)  21.5 us
  transfers between devices with their start and end apart: 52, of which 20 were waited for; matrix products, arithmetic and copies ran while one was open for 25% of the time, Pallas kernels for 27%

profile of v1, /device:TPU:1, one launch (start us, length us, event | category | flops | bytes accessed | tf_op | source)
XLA Modules:
  0.0 471.6 jit_solution(7806030501192734920)
XLA Ops:
  51.1 13.5 %collective-permute-done.9.refs_3_ = bf16[512,768]{1,0:T(8,128)(2,1)S(1)} collective-permute-done((bf16[512,768]{1,0:T(8,128)(2,1)S(1)}, bf16[512,768]{1,0:T(8,128)(2,1)S(1)}, u32[]{:S(2)}, u32[]{:S(2)}) %collective-permute-start.9) | collective-permute-done | bytes 786464 | tf_op jit(solution)/shard_map/ppermute | solution.py:793
  66.0 5.5 %collective-permute-start.10 = (bf16[1024,512]{1,0:T(8,128)(2,1)}, bf16[1024,512]{1,0:T(8,128)(2,1)}, u32[]{:S(2)}, u32[]{:S(2)}) collective-permute-start(bf16[1024,512]{1,0:T(8,128)(2,1)} %maximum_maximum_fusion.1), channel_id=1, source_target_pairs={{0,1},{1,0},{2,3},{3,2},{4,5},{5,4},{6,7},{7,6},{8,9},{9,8},{10,11... | collective-permute-start | bytes 3145736 | tf_op jit(solution)/shard_map/ppermute | solution.py:799
  74.1 7.4 %shard_map.247 = (bf16[512,1024]{1,0:T(8,128)(2,1)}, f32[512,1024]{1,0:T(8,128)}, bf16[8,2,256,128]{3,2,1,0:T(8,128)(2,1)}) custom-call(s32[1]{0:T(128)} %bitcast.core_ref, bf16[512,1024]{1,0:T(8,128)(2,1)} %get-tuple-element.213.x_ref, f32[1,1024]{1,0:T(1,128)} %bitcast.185, f32[1,128]{1,0:T(1,128)} %maximum_bitcast_fusion.1.gain_ref, ...), custom_call_target="tpu_custom_call" | custom-call | flops 1073741824 | bytes 8388608 | tf_op jit(solution)/shard_map/pallas_call | solution.py:99
  81.5 7.3 %collective-permute-done.13 = bf16[128,1792]{1,0:T(8,128)(2,1)S(1)} collective-permute-done((bf16[128,1792]{1,0:T(8,128)(2,1)S(1)}, bf16[128,1792]{1,0:T(8,128)(2,1)S(1)}, u32[]{:S(2)}, u32[]{:S(2)}) %collective-permute-start.13) | collective-permute-done | bytes 458784 | tf_op jit(solution)/shard_map/ppermute | solution.py:793
  89.6 5.6 %all-to-all-start = ((bf16[16,256,128]{2,1,0:T(8,128)(2,1)}), bf16[16,256,128]{2,1,0:T(8,128)(2,1)}, u32[]{:S(2)}, u32[]{:S(2)}) async-start(bf16[16,256,128]{2,1,0:T(8,128)(2,1)} %bitcast.179), calls=%async_computation | async-start | bytes 2097152 | tf_op jit(solution)/shard_map/all_to_all | solution.py:870
  101.9 8.6 %fusion.36.wo_ref = bf16[1024,1024]{1,0:T(8,128)(2,1)} fusion(s32[1024]{0:T(1024)} %copy-done.91, s32[1024]{0:T(1024)} %copy-done.92, bf16[1024,1024]{1,0:T(8,128)(2,1)} %copy-done.10, bf16[1024,512]{1,0:T(8,128)(2,1)} %collective-permute-done.10, bf16[256,256]{1,0:T(8,128)(2,1)} %copy-done.71, bf16[256,256]{1,0:T(8,128)(2,1)} %copy-done.69, ...), kind=kOutput, calls=%fused_computation.44 | convolution fusion | flops 4328521728 | bytes 6299649 | tf_op jit(solution)/shard_map/dot_general | solution.py:31
  123.2 22.3 %shard_map.248 = (bf16[2048,128]{1,0:T(8,128)(2,1)}, f32[64,4096]{1,0:T(8,128)}, f32[1,4096]{1,0:T(1,128)}) custom-call(s32[1]{0:T(128)} %bitcast.core_ref, s32[32]{0:T(128)} %get-tuple-element.163.kslot_ref, s32[32]{0:T(128)} %get-tuple-element.162.qslot_ref, s32[4,8]{1,0:T(4,128)} %pad_add_fusion.lims_ref, bf16[4096,128]{1,0:T(8,128)(2,1)} %bitcast.66.q_ref.own_ref, ...), custom_call_target="tpu_custom_call" | custom-call | flops 8589934592 | bytes 8388608 | tf_op jit(solution)/shard_map/pallas_call | solution.py:248
  145.5 6.1 %all-to-all-start.1 = ((bf16[16,128,128]{2,1,0:T(8,128)(2,1)}), bf16[16,128,128]{2,1,0:T(8,128)(2,1)}, u32[]{:S(2)}, u32[]{:S(2)}) async-start(bf16[16,128,128]{2,1,0:T(8,128)(2,1)} %bitcast.181), calls=%async_computation.1 | async-start | bytes 1048576 | tf_op jit(solution)/shard_map/all_to_all | solution.py:870
  170.4 5.8 %shard_map.249 = (f32[512,1024]{1,0:T(8,128)}, bf16[512,1024]{1,0:T(8,128)(2,1)}, bf16[512,1024]{1,0:T(8,128)(2,1)}, bf16[256,1024]{1,0:T(8,128)(2,1)}) custom-call(s32[1]{0:T(128)} %bitcast.core_ref, bf16[2048,128]{1,0:T(8,128)(2,1)} %bitcast.70.own_ref, bf16[2048,128]{1,0:T(8,128)(2,1)} %copy-done.68, bf16[512,1024]{1,0:T(8,128)(2,1)} %convolution_convert_fusion.1.x_ref, ...), custom_call_target="tpu_custom_call" | custom-call | flops 1073741824 | bytes 10485760 | tf_op jit(solution)/shard_map/pallas_call | solution.py:669
  177.6 11.6 %collective-permute-done.19 = bf16[256,1024]{1,0:T(8,128)(2,1)S(1)} collective-permute-done((bf16[256,1024]{1,0:T(8,128)(2,1)}, bf16[256,1024]{1,0:T(8,128)(2,1)S(1)}, u32[]{:S(2)}, u32[]{:S(2)}) %collective-permute-start.19) | collective-permute-done | bytes 524320 | tf_op jit(solution)/shard_map/ppermute | solution.py:793
  205.3 13.2 %shard_map.252 = (bf16[512,1152]{1,0:T(8,128)(2,1)}, bf16[512,1152]{1,0:T(8,128)(2,1)}, bf16[512,1152]{1,0:T(8,128)(2,1)}, f32[512,1024]{1,0:T(8,128)}, bf16[512...) custom-call(bf16[512,1024]{1,0:T(8,128)(2,1)} %pad_maximum_fusion.3.n_ref, bf16[512,1024]{1,0:T(8,128)(2,1)} %copy-done.31, ...), custom_call_target="tpu_custom_call" | custom-call | flops 7247757312 | bytes 16777216 | tf_op jit(solution)/shard_map/pallas_call | solution.py:435
  225.1 13.8 %shard_map.250 = (bf16[512,1152]{1,0:T(8,128)(2,1)}, bf16[512,1152]{1,0:T(8,128)(2,1)}, bf16[512,1152]{1,0:T(8,128)(2,1)}, f32[512,1024]{1,0:T(8,128)}, bf16[512...) custom-call(bf16[512,1024]{1,0:T(8,128)(2,1)} %get-tuple-element.100.n_ref, bf16[512,1024]{1,0:T(8,128)(2,1)} %copy-done.7, ...), custom_call_target="tpu_custom_call" | custom-call | flops 7247757312 | bytes 16777216 | tf_op jit(solution)/shard_map/pallas_call | solution.py:435
  246.4 6.8 %shard_map.253 = (f32[512,1024]{1,0:T(8,128)}, bf16[512,1024]{1,0:T(8,128)(2,1)}, f32[1,1024]{1,0:T(1,128)}, bf16[2048,128]{1,0:T(8,128)(2,1)}) custom-call(s32[1]{0:T(128)} %bitcast.core_ref, bf16[512,1024]{1,0:T(8,128)(2,1)} %get-tuple-element.112.back_ref, bf16[512,1024]{1,0:T(8,128)(2,1)} %copy-done.60, bf16[256,1024]{1,0:T(8,128)(2,1)} %copy-done.77, ...), custom_call_target="tpu_custom_call" | custom-call | flops 536870912 | bytes 10485760 | tf_op jit(solution)/shard_map/pallas_call | solution.py:712
  253.1 5.5 %all-to-all-start.2 = ((bf16[16,128,128]{2,1,0:T(8,128)(2,1)}), bf16[16,128,128]{2,1,0:T(8,128)(2,1)}, u32[]{:S(2)}, u32[]{:S(2)}) async-start(bf16[16,128,128]{2,1,0:T(8,128)(2,1)} %bitcast.180), calls=%async_computation.2 | async-start | bytes 1048576 | tf_op jit(solution)/shard_map/all_to_all | solution.py:870
  260.8 14.6 %shard_map.254 = (bf16[512,1792]{1,0:T(8,128)(2,1)}, bf16[512,1792]{1,0:T(8,128)(2,1)}, bf16[512,1664]{1,0:T(8,128)(2,1)}, bf16[512,1664]{1,0:T(8,128)(2,1)}) custom-call(bf16[1024,512]{1,0:T(8,128)(2,1)} %get-tuple-element.116.refs_0_, bf16[1024,512]{1,0:T(8,128)(2,1)} %get-tuple-element.107.refs_1_, bf16[1024,512]{1,0:T(8,128)(2,1)} %get-tuple-element.117.refs_2_, ...), custom_call_target="tpu_custom_call" | custom-call | flops 7247757312 | bytes 16777216 | tf_op jit(solution)/shard_map/pallas_call | solution.py:513
  283.1 35.4 %shard_map.255 = (f32[4096,128]{1,0:T(8,128)}, f32[4096,128]{1,0:T(8,128)}, bf16[4096,128]{1,0:T(8,128)(2,1)}) custom-call(s32[1]{0:T(128)} %bitcast.core_ref, s32[32]{0:T(128)} %get-tuple-element.163.kslot_ref, s32[32]{0:T(128)} %get-tuple-element.162.qslot_ref, s32[4,8]{1,0:T(4,128)} %pad_add_fusion.lims_ref, bf16[4096,128]{1,0:T(8,128)(2,1)} %bitcast.66.q_ref.own_ref, ...), custom_call_target="tpu_custom_call" | custom-call | flops 17179869184 | bytes 8388608 | tf_op jit(solution)/shard_map/pallas_call | solution.py:358
  325.3 6.4 %shard_map.257 = bf16[1024,512]{1,0:T(8,128)(2,1)} custom-call(s32[1]{0:T(128)} %bitcast.core_ref, bf16[512,1024]{1,0:T(8,128)(2,1)} %get-tuple-element.136.attn_ref, bf16[512,1024]{1,0:T(8,128)(2,1)} %get-tuple-element.137.grad_ref, bf16[1024,1024]{1,0:T(8,128)(2,1)} %get-tuple-element.193.select_ref, bf16[1024,1024]{1,0:T(8,128)(2,1)} %get-tuple-element.111.unperm_ref), custom_call_target="tpu_custom_call" | custom-call | flops 4294967296 | bytes 8388608 | tf_op jit(solution)/shard_map/pallas_call | solution.py:472
  356.2 7.7 %all-to-all-done.3 = bf16[16,256,128]{2,1,0:T(8,128)(2,1)} async-done(((bf16[16,256,128]{2,1,0:T(8,128)(2,1)}), bf16[16,256,128]{2,1,0:T(8,128)(2,1)}, u32[]{:S(2)}, u32[]{:S(2)}) %all-to-all-start.3) | async-done | bytes 1048608 | tf_op jit(solution)/shard_map/all_to_all | solution.py:870
  363.9 8.2 %shard_map.256 = (bf16[512,1024]{1,0:T(8,128)(2,1)}, f32[8,8,128]{2,1,0:T(8,128)}) custom-call(s32[1]{0:T(128)} %bitcast.core_ref, bf16[8,2,256,128]{3,2,1,0:T(8,128)(2,1)} %bitcast.76.grad_ref, f32[512,1024]{1,0:T(8,128)} %get-tuple-element.132.raw_ref, f32[1,128]{1,0:T(1,128)} %maximum_bitcast_fusion.1.gain_ref, f32[256,128]{1,0:T(8,128)} %pad_maximum_fusion.25.cos_ref, ...), custom_call_target="tpu_custom_call" | custom-call | flops 16777216 | bytes 8388608 | tf_op jit(solution)/shard_map/pallas_call | solution.py:138
  383.3 9.7 %collective-permute-done.31 = bf16[512,768]{1,0:T(8,128)(2,1)S(1)} collective-permute-done((bf16[512,768]{1,0:T(8,128)(2,1)S(1)}, bf16[512,768]{1,0:T(8,128)(2,1)S(1)}, u32[]{:S(2)}, u32[]{:S(2)}) %collective-permute-start.31) | collective-permute-done | bytes 786464 | tf_op jit(solution)/shard_map/ppermute | solution.py:793
  407.4 5.1 %all-to-all-start.4 = ((f32[16,8,256]{2,1,0:T(8,128)}), f32[16,8,256]{2,1,0:T(8,128)S(1)}, u32[]{:S(2)}, u32[]{:S(2)}) async-start(f32[16,8,256]{2,1,0:T(8,128)} %broadcast_in_dim.174), calls=%async_computation.4 | async-start | bytes 262144 | tf_op jit(solution)/shard_map/all_to_all | solution.py:1154
  421.6 9.4 %collective-permute-done.43 = bf16[128,1664]{1,0:T(8,128)(2,1)} collective-permute-done((bf16[128,1664]{1,0:T(8,128)(2,1)}, bf16[128,1664]{1,0:T(8,128)(2,1)}, u32[]{:S(2)}, u32[]{:S(2)}) %collective-permute-start.43) | collective-permute-done | bytes 426016 | tf_op jit(solution)/shard_map/ppermute | solution.py:793
  432.4 8.4 %collective-permute-done.40 = bf16[128,1792]{1,0:T(8,128)(2,1)} collective-permute-done((bf16[128,1792]{1,0:T(8,128)(2,1)}, bf16[128,1792]{1,0:T(8,128)(2,1)}, u32[]{:S(2)}, u32[]{:S(2)}) %collective-permute-start.40) | collective-permute-done | bytes 458784 | tf_op jit(solution)/shard_map/ppermute | solution.py:793
  452.1 5.6 %collective-permute-done.44 = bf16[64,3456]{1,0:T(8,128)(2,1)S(1)} collective-permute-done((bf16[64,3456]{1,0:T(8,128)(2,1)S(1)}, bf16[64,3456]{1,0:T(8,128)(2,1)S(1)}, u32[]{:S(2)}, u32[]{:S(2)}) %collective-permute-start.44) | collective-permute-done | bytes 442400 | tf_op jit(solution)/shard_map/ppermute | solution.py:793
  (471 shorter events, 225.4 us)
Async XLA Ops:
  5.2 23.8 %collective-permute-start.6 = (bf16[2,256,1024]{2,1,0:T(8,128)(2,1)}, bf16[2,256,1024]{2,1,0:T(8,128)(2,1)}, u32[]{:S(2)}, u32[]{:S(2)}) collective-permute-start(bf16[2,256,1024]{2,1,0:T(8,128)(2,1)} %pad_maximum_fusion.2), channel_id=1, source_target_pairs={{0,1},{1,0},{2,3},{3,2},{4,5},{5,4},{6,7},{7,6},{8,9},{9,8},{10,11... | collective-permute-start | bytes 3145736 | tf_op jit(solution)/shard_map/ppermute | solution.py:799
  48.4 33.1 %collective-permute-start.16 = (bf16[128,1664]{1,0:T(8,128)(2,1)S(1)}, bf16[128,1664]{1,0:T(8,128)(2,1)S(1)}, u32[]{:S(2)}, u32[]{:S(2)}) collective-permute-start(bf16[128,1664]{1,0:T(8,128)(2,1)S(1)} %maximum_select_fusion.11), channel_id=1, source_target_pairs={{0,16},{2,18},{4,20},{6,22},{8,24},{10,26},{12,28},{14,30},{16,0},... | collective-permute-start | bytes 1277960 | tf_op jit(solution)/shard_map/ppermute | solution.py:793
  49.6 39.2 %collective-permute-start.13 = (bf16[128,1792]{1,0:T(8,128)(2,1)S(1)}, bf16[128,1792]{1,0:T(8,128)(2,1)S(1)}, u32[]{:S(2)}, u32[]{:S(2)}) collective-permute-start(bf16[128,1792]{1,0:T(8,128)(2,1)S(1)} %maximum_select_fusion.10), channel_id=1, source_target_pairs={{0,16},{2,18},{4,20},{6,22},{8,24},{10,26},{12,28},{14,30},{16,0},... | collective-permute-start | bytes 1376264 | tf_op jit(solution)/shard_map/ppermute | solution.py:793
  66.0 35.9 %collective-permute-start.10 = (bf16[1024,512]{1,0:T(8,128)(2,1)}, bf16[1024,512]{1,0:T(8,128)(2,1)}, u32[]{:S(2)}, u32[]{:S(2)}) collective-permute-start(bf16[1024,512]{1,0:T(8,128)(2,1)} %maximum_maximum_fusion.1), channel_id=1, source_target_pairs={{0,1},{1,0},{2,3},{3,2},{4,5},{5,4},{6,7},{7,6},{8,9},{9,8},{10,11... | collective-permute-start | bytes 3145736 | tf_op jit(solution)/shard_map/ppermute | solution.py:799
  89.6 28.7 %all-to-all-start = ((bf16[16,256,128]{2,1,0:T(8,128)(2,1)}), bf16[16,256,128]{2,1,0:T(8,128)(2,1)}, u32[]{:S(2)}, u32[]{:S(2)}) async-start(bf16[16,256,128]{2,1,0:T(8,128)(2,1)} %bitcast.179), calls=%async_computation | async-start | bytes 2097152 | tf_op jit(solution)/shard_map/all_to_all | solution.py:870
  97.2 61.5 %collective-permute-start.17 = (bf16[256,1664]{1,0:T(8,128)(2,1)}, bf16[256,1664]{1,0:T(8,128)(2,1)}, u32[]{:S(2)}, u32[]{:S(2)}) collective-permute-start(bf16[256,1664]{1,0:T(8,128)(2,1)} %pad_maximum_fusion.10), channel_id=1, source_target_pairs={{0,4},{2,6},{4,0},{6,2},{8,12},{10,14},{12,8},{14,10},{16,20},{18,... | collective-permute-start | bytes 2555912 | tf_op jit(solution)/shard_map/ppermute | solution.py:793
  100.7 61.7 %collective-permute-start.14 = (bf16[256,1792]{1,0:T(8,128)(2,1)}, bf16[256,1792]{1,0:T(8,128)(2,1)}, u32[]{:S(2)}, u32[]{:S(2)}) collective-permute-start(bf16[256,1792]{1,0:T(8,128)(2,1)} %pad_maximum_fusion.6), channel_id=1, source_target_pairs={{0,8},{2,10},{4,12},{6,14},{8,0},{10,2},{12,4},{14,6},{16,24},{18,... | collective-permute-start | bytes 2752520 | tf_op jit(solution)/shard_map/ppermute | solution.py:793
  161.2 39.1 %collective-permute-start.18 = (bf16[512,1664]{1,0:T(8,128)(2,1)}, bf16[512,1664]{1,0:T(8,128)(2,1)}, u32[]{:S(2)}, u32[]{:S(2)}) collective-permute-start(bf16[512,1664]{1,0:T(8,128)(2,1)} %pad_maximum_fusion.1.refs_2_), channel_id=1, source_target_pairs={{0,8},{2,10},{4,12},{6,14},{8,0},{10,2},{12,4},{14,6},{16,24},{18,... | collective-permute-start | bytes 5111816 | tf_op jit(solution)/shard_map/ppermute | solution.py:793
  164.9 40.3 %collective-permute-start.15 = (bf16[512,1792]{1,0:T(8,128)(2,1)}, bf16[512,1792]{1,0:T(8,128)(2,1)}, u32[]{:S(2)}, u32[]{:S(2)}) collective-permute-start(bf16[512,1792]{1,0:T(8,128)(2,1)} %pad_maximum_fusion.refs_0_), channel_id=1, source_target_pairs={{0,4},{2,6},{4,0},{6,2},{8,12},{10,14},{12,8},{14,10},{16,20},{18,... | collective-permute-start | bytes 5505032 | tf_op jit(solution)/shard_map/ppermute | solution.py:793
  244.1 34.0 %collective-permute-start.23 = (bf16[512,1024]{1,0:T(8,128)(2,1)}, bf16[512,1024]{1,0:T(8,128)(2,1)}, u32[]{:S(2)}, u32[]{:S(2)}) collective-permute-start(bf16[512,1024]{1,0:T(8,128)(2,1)} %pad_maximum_fusion.4), channel_id=1, source_target_pairs={{0,1},{1,0},{2,3},{3,2},{4,5},{5,4},{6,7},{7,6},{8,9},{9,8},{10,11... | collective-permute-start | bytes 3145736 | tf_op jit(solution)/shard_map/ppermute | solution.py:799
  253.1 30.0 %all-to-all-start.2 = ((bf16[16,128,128]{2,1,0:T(8,128)(2,1)}), bf16[16,128,128]{2,1,0:T(8,128)(2,1)}, u32[]{:S(2)}, u32[]{:S(2)}) async-start(bf16[16,128,128]{2,1,0:T(8,128)(2,1)} %bitcast.180), calls=%async_computation.2 | async-start | bytes 1048576 | tf_op jit(solution)/shard_map/all_to_all | solution.py:870
  275.5 72.0 %collective-permute-start.41 = (bf16[512,1664]{1,0:T(8,128)(2,1)}, bf16[512,1664]{1,0:T(8,128)(2,1)}, u32[]{:S(2)}, u32[]{:S(2)}) collective-permute-start(bf16[512,1664]{1,0:T(8,128)(2,1)} %get-tuple-element.125), channel_id=1, source_target_pairs={{0,8},{2,10},{4,12},{6,14},{8,0},{10,2},{12,4},{14,6},{16,24},{18,... | collective-permute-start | bytes 5111816 | tf_op jit(solution)/shard_map/ppermute | solution.py:793
  277.0 74.8 %collective-permute-start.38 = (bf16[512,1792]{1,0:T(8,128)(2,1)}, bf16[512,1792]{1,0:T(8,128)(2,1)}, u32[]{:S(2)}, u32[]{:S(2)}) collective-permute-start(bf16[512,1792]{1,0:T(8,128)(2,1)} %get-tuple-element.124), channel_id=1, source_target_pairs={{0,4},{2,6},{4,0},{6,2},{8,12},{10,14},{12,8},{14,10},{16,20},{18,... | collective-permute-start | bytes 5505032 | tf_op jit(solution)/shard_map/ppermute | solution.py:793
  281.9 38.3 %collective-permute-start.24 = (bf16[256,1024]{1,0:T(8,128)(2,1)}, bf16[256,1024]{1,0:T(8,128)(2,1)}, u32[]{:S(2)}, u32[]{:S(2)}) collective-permute-start(bf16[256,1024]{1,0:T(8,128)(2,1)} %fusion.45), channel_id=1, source_target_pairs={{0,2},{2,0},{4,6},{6,4},{8,10},{10,8},{12,14},{14,12},{16,18},{18,... | collective-permute-start | bytes 1572872 | tf_op jit(solution)/shard_map/ppermute | solution.py:793
  336.1 27.8 %all-to-all-start.3 = ((bf16[16,256,128]{2,1,0:T(8,128)(2,1)}), bf16[16,256,128]{2,1,0:T(8,128)(2,1)}, u32[]{:S(2)}, u32[]{:S(2)}) async-start(bf16[16,256,128]{2,1,0:T(8,128)(2,1)} %bitcast.176), calls=%async_computation.3 | async-start | bytes 2097152 | tf_op jit(solution)/shard_map/all_to_all | solution.py:870
  350.6 46.4 %collective-permute-start.42 = (bf16[256,1664]{1,0:T(8,128)(2,1)}, bf16[256,1664]{1,0:T(8,128)(2,1)}, u32[]{:S(2)}, u32[]{:S(2)}) collective-permute-start(bf16[256,1664]{1,0:T(8,128)(2,1)} %get-tuple-element.169), channel_id=1, source_target_pairs={{0,4},{2,6},{4,0},{6,2},{8,12},{10,14},{12,8},{14,10},{16,20},{18,... | collective-permute-start | bytes 2555912 | tf_op jit(solution)/shard_map/ppermute | solution.py:793
  355.0 47.4 %collective-permute-start.39 = (bf16[256,1792]{1,0:T(8,128)(2,1)}, bf16[256,1792]{1,0:T(8,128)(2,1)}, u32[]{:S(2)}, u32[]{:S(2)}) collective-permute-start(bf16[256,1792]{1,0:T(8,128)(2,1)} %get-tuple-element.167), channel_id=1, source_target_pairs={{0,8},{2,10},{4,12},{6,14},{8,0},{10,2},{12,4},{14,6},{16,24},{18,... | collective-permute-start | bytes 2752520 | tf_op jit(solution)/shard_map/ppermute | solution.py:793
  380.9 23.3 %collective-permute-start.30 = (f32[256,1024]{1,0:T(8,128)S(1)}, f32[256,1024]{1,0:T(8,128)S(1)}, u32[]{:S(2)}, u32[]{:S(2)}) collective-permute-start(f32[256,1024]{1,0:T(8,128)S(1)} %slice_select_fusion.2), channel_id=1, source_target_pairs={{0,1},{1,0},{2,3},{3,2},{4,5},{5,4},{6,7},{7,6},{8,9},{9,8},{10,11... | collective-permute-start | bytes 3145736 | tf_op jit(solution)/shard_map/ppermute | solution.py:799
  394.0 22.7 %collective-permute-start.32 = (bf16[256,768]{1,0:T(8,128)(2,1)}, bf16[256,768]{1,0:T(8,128)(2,1)}, u32[]{:S(2)}, u32[]{:S(2)}) collective-permute-start(bf16[256,768]{1,0:T(8,128)(2,1)} %add_convert_fusion.12), channel_id=1, source_target_pairs={{0,2},{2,0},{4,6},{6,4},{8,10},{10,8},{12,14},{14,12},{16,18},{18,... | collective-permute-start | bytes 1179656 | tf_op jit(solution)/shard_map/ppermute | solution.py:793
  396.4 21.6 %collective-permute-start.34 = (bf16[256,768]{1,0:T(8,128)(2,1)}, bf16[256,768]{1,0:T(8,128)(2,1)}, u32[]{:S(2)}, u32[]{:S(2)}) collective-permute-start(bf16[256,768]{1,0:T(8,128)(2,1)} %add_convert_fusion.10), channel_id=1, source_target_pairs={{0,4},{2,6},{4,0},{6,2},{8,12},{10,14},{12,8},{14,10},{16,20},{18,... | collective-permute-start | bytes 1179656 | tf_op jit(solution)/shard_map/ppermute | solution.py:793
  398.9 32.2 %collective-permute-start.43 = (bf16[128,1664]{1,0:T(8,128)(2,1)}, bf16[128,1664]{1,0:T(8,128)(2,1)}, u32[]{:S(2)}, u32[]{:S(2)}) collective-permute-start(bf16[128,1664]{1,0:T(8,128)(2,1)} %add_convert_fusion.8), channel_id=1, source_target_pairs={{0,16},{2,18},{4,20},{6,22},{8,24},{10,26},{12,28},{14,30},{16,0},... | collective-permute-start | bytes 1277960 | tf_op jit(solution)/shard_map/ppermute | solution.py:793
  404.2 36.7 %collective-permute-start.40 = (bf16[128,1792]{1,0:T(8,128)(2,1)}, bf16[128,1792]{1,0:T(8,128)(2,1)}, u32[]{:S(2)}, u32[]{:S(2)}) collective-permute-start(bf16[128,1792]{1,0:T(8,128)(2,1)} %add_convert_fusion.6), channel_id=1, source_target_pairs={{0,16},{2,18},{4,20},{6,22},{8,24},{10,26},{12,28},{14,30},{16,0},... | collective-permute-start | bytes 1376264 | tf_op jit(solution)/shard_map/ppermute | solution.py:793
  407.4 35.3 %all-to-all-start.4 = ((f32[16,8,256]{2,1,0:T(8,128)}), f32[16,8,256]{2,1,0:T(8,128)S(1)}, u32[]{:S(2)}, u32[]{:S(2)}) async-start(f32[16,8,256]{2,1,0:T(8,128)} %broadcast_in_dim.174), calls=%async_computation.4 | async-start | bytes 262144 | tf_op jit(solution)/shard_map/all_to_all | solution.py:1154
  420.2 28.2 %collective-permute-start.35 = (bf16[128,1536]{1,0:T(8,128)(2,1)}, bf16[128,1536]{1,0:T(8,128)(2,1)}, u32[]{:S(2)}, u32[]{:S(2)}) collective-permute-start(bf16[128,1536]{1,0:T(8,128)(2,1)} %fusion.75), channel_id=1, source_target_pairs={{0,8},{2,10},{4,12},{6,14},{8,0},{10,2},{12,4},{14,6},{16,24},{18,... | collective-permute-start | bytes 1179656 | tf_op jit(solution)/shard_map/ppermute | solution.py:793
  (131 other events, 1096.6 us)

commit v2 on v1

--- a/solution.py
+++ b/solution.py
@@ -48,9 +48,12 @@
 
 
 def half_sums(value, low):
-    total = jnp.sum(value, axis=-1, keepdims=True)
-    first = jnp.sum(jnp.where(low, value, 0.0), axis=-1, keepdims=True)
-    return jnp.where(low, first, total - first)
+    shape = (LANES, LANES)
+    same = lax.broadcasted_iota(I32, shape, 0) // HEAD == lax.broadcasted_iota(I32, shape, 1) // HEAD
+    ones = jnp.where(same, 1.0, 0.0).astype(BF)
+    high = value.astype(BF)
+    rest = (value - high.astype(F32)).astype(BF)
+    return dot(high, ones) + dot(rest, ones)
 
 
 def half_turn(value):

time: 478 us -> 483 us (1.010)
  Pallas kernels: 145 us -> 150 us
  transfers between devices with their start and end apart: 52 -> 52, of which waited for: 20 -> 21; matrix products, arithmetic and copies ran while one was open for 25% -> 25% of each run, Pallas kernels for 27% -> 27%
where the time goes in v2:
time: 483 us; the launch traced here: 478 us
  Pallas kernels  150 us (31%)
  waiting for transfers between devices  103 us (21%)
  starting transfers between devices  93.3 us (19%)
  other arithmetic  61.6 us (13%)
  matrix products  38.6 us (8%)
  local copies, waits for them, and re-layouts  29.9 us (6%)
    ppermute x30, waiting for transfers between devices, ctx_send(): return lax.ppermute(value, 'ctx', pairs)  92.6 us
    ppermute x30, starting transfers between devices, ctx_send(): return lax.ppermute(value, 'ctx', pairs)  40.3 us
    pallas_call x1, Pallas kernels, attend_back(): pl.pallas_call(attend_back_kernel, in_specs=[in_smem()] * 4 + [in_vmem()]...  39.8 us
    dot_general x16, matrix products, dot(): return lax.dot_general(a, b, dims, preferred_element_type=F32)  36.7 us
    pallas_call x2, Pallas kernels, feed(): pl.pallas_call(functools.partial(feed_kernel, len(parts[0]), chunk, order...  27 us
    ppermute x17, starting transfers between devices, core_swap(): return lax.ppermute(value, 'wt', [(0, 1), (1, 0)])  26.2 us
    pallas_call x1, Pallas kernels, attend(): pl.pallas_call(attend_kernel, in_specs=[in_smem()] * 4 + [in_vmem()] * 5,...  25 us
    all_to_all x4, starting transfers between devices, swap_heads(): lax.all_to_all(value, 'ctx', 0, 0, axis_index_groups=a2a_groups, tiled=True)  21.4 us
  transfers between devices with their start and end apart: 52, of which 21 were waited for; matrix products, arithmetic and copies ran while one was open for 25% of the time, Pallas kernels for 27%

profile of v2, /device:TPU:1, one launch (start us, length us, event | category | flops | bytes accessed | tf_op | source)
XLA Modules:
  0.0 478.4 jit_solution(12796346405031729972)
XLA Ops:
  18.1 5.1 %collective-permute-done.1 = bf16[64,1664]{1,0:T(8,128)(2,1)S(1)} collective-permute-done((bf16[64,1664]{1,0:T(8,128)(2,1)S(1)}, bf16[64,1664]{1,0:T(8,128)(2,1)S(1)}, u32[]{:S(2)}, u32[]{:S(2)}) %collective-permute-start.1) | collective-permute-done | bytes 213024 | tf_op jit(solution)/shard_map/ppermute | solution.py:796
  51.1 13.5 %collective-permute-done.9.refs_3_ = bf16[512,768]{1,0:T(8,128)(2,1)S(1)} collective-permute-done((bf16[512,768]{1,0:T(8,128)(2,1)S(1)}, bf16[512,768]{1,0:T(8,128)(2,1)S(1)}, u32[]{:S(2)}, u32[]{:S(2)}) %collective-permute-start.9) | collective-permute-done | bytes 786464 | tf_op jit(solution)/shard_map/ppermute | solution.py:796
  66.0 5.5 %collective-permute-start.10 = (bf16[1024,512]{1,0:T(8,128)(2,1)}, bf16[1024,512]{1,0:T(8,128)(2,1)}, u32[]{:S(2)}, u32[]{:S(2)}) collective-permute-start(bf16[1024,512]{1,0:T(8,128)(2,1)} %maximum_maximum_fusion.1), channel_id=1, source_target_pairs={{0,1},{1,0},{2,3},{3,2},{4,5},{5,4},{6,7},{7,6},{8,9},{9,8},{10,11... | collective-permute-start | bytes 3145736 | tf_op jit(solution)/shard_map/ppermute | solution.py:802
  74.1 6.1 %shard_map.247 = (bf16[512,1024]{1,0:T(8,128)(2,1)}, f32[512,1024]{1,0:T(8,128)}, bf16[8,2,256,128]{3,2,1,0:T(8,128)(2,1)}) custom-call(s32[1]{0:T(128)} %bitcast.core_ref, bf16[512,1024]{1,0:T(8,128)(2,1)} %get-tuple-element.213.x_ref, f32[1,1024]{1,0:T(1,128)} %bitcast.185, f32[1,128]{1,0:T(1,128)} %maximum_bitcast_fusion.1.gain_ref, ...), custom_call_target="tpu_custom_call" | custom-call | flops 1073741824 | bytes 8388608 | tf_op jit(solution)/shard_map/pallas_call | solution.py:102
  80.2 8.6 %collective-permute-done.13 = bf16[128,1792]{1,0:T(8,128)(2,1)S(1)} collective-permute-done((bf16[128,1792]{1,0:T(8,128)(2,1)S(1)}, bf16[128,1792]{1,0:T(8,128)(2,1)S(1)}, u32[]{:S(2)}, u32[]{:S(2)}) %collective-permute-start.13) | collective-permute-done | bytes 458784 | tf_op jit(solution)/shard_map/ppermute | solution.py:796
  89.6 5.6 %all-to-all-start = ((bf16[16,256,128]{2,1,0:T(8,128)(2,1)}), bf16[16,256,128]{2,1,0:T(8,128)(2,1)}, u32[]{:S(2)}, u32[]{:S(2)}) async-start(bf16[16,256,128]{2,1,0:T(8,128)(2,1)} %bitcast.179), calls=%async_computation | async-start | bytes 2097152 | tf_op jit(solution)/shard_map/all_to_all | solution.py:873
  102.1 8.6 %fusion.36.wo_ref = bf16[1024,1024]{1,0:T(8,128)(2,1)} fusion(s32[1024]{0:T(1024)} %copy-done.91, s32[1024]{0:T(1024)} %copy-done.92, bf16[1024,1024]{1,0:T(8,128)(2,1)} %copy-done.10, bf16[1024,512]{1,0:T(8,128)(2,1)} %collective-permute-done.10, bf16[256,256]{1,0:T(8,128)(2,1)} %copy-done.71, bf16[256,256]{1,0:T(8,128)(2,1)} %copy-done.69, ...), kind=kOutput, calls=%fused_computation.44 | convolution fusion | flops 4328521728 | bytes 6299649 | tf_op jit(solution)/shard_map/dot_general | solution.py:31
  123.2 25.0 %shard_map.248 = (bf16[2048,128]{1,0:T(8,128)(2,1)}, f32[64,4096]{1,0:T(8,128)}, f32[1,4096]{1,0:T(1,128)}) custom-call(s32[1]{0:T(128)} %bitcast.core_ref, s32[32]{0:T(128)} %get-tuple-element.163.kslot_ref, s32[32]{0:T(128)} %get-tuple-element.162.qslot_ref, s32[4,8]{1,0:T(4,128)} %pad_add_fusion.lims_ref, bf16[4096,128]{1,0:T(8,128)(2,1)} %bitcast.66.q_ref.own_ref, ...), custom_call_target="tpu_custom_call" | custom-call | flops 8589934592 | bytes 8388608 | tf_op jit(solution)/shard_map/pallas_call | solution.py:251
  148.2 6.0 %all-to-all-start.1 = ((bf16[16,128,128]{2,1,0:T(8,128)(2,1)}), bf16[16,128,128]{2,1,0:T(8,128)(2,1)}, u32[]{:S(2)}, u32[]{:S(2)}) async-start(bf16[16,128,128]{2,1,0:T(8,128)(2,1)} %bitcast.181), calls=%async_computation.1 | async-start | bytes 1048576 | tf_op jit(solution)/shard_map/all_to_all | solution.py:873
  173.1 5.8 %shard_map.249 = (f32[512,1024]{1,0:T(8,128)}, bf16[512,1024]{1,0:T(8,128)(2,1)}, bf16[512,1024]{1,0:T(8,128)(2,1)}, bf16[256,1024]{1,0:T(8,128)(2,1)}) custom-call(s32[1]{0:T(128)} %bitcast.core_ref, bf16[2048,128]{1,0:T(8,128)(2,1)} %bitcast.70.own_ref, bf16[2048,128]{1,0:T(8,128)(2,1)} %copy-done.68, bf16[512,1024]{1,0:T(8,128)(2,1)} %convolution_convert_fusion.1.x_ref, ...), custom_call_target="tpu_custom_call" | custom-call | flops 1073741824 | bytes 10485760 | tf_op jit(solution)/shard_map/pallas_call | solution.py:672
  180.2 11.6 %collective-permute-done.19 = bf16[256,1024]{1,0:T(8,128)(2,1)S(1)} collective-permute-done((bf16[256,1024]{1,0:T(8,128)(2,1)}, bf16[256,1024]{1,0:T(8,128)(2,1)S(1)}, u32[]{:S(2)}, u32[]{:S(2)}) %collective-permute-start.19) | collective-permute-done | bytes 524320 | tf_op jit(solution)/shard_map/ppermute | solution.py:796
  207.9 13.2 %shard_map.252 = (bf16[512,1152]{1,0:T(8,128)(2,1)}, bf16[512,1152]{1,0:T(8,128)(2,1)}, bf16[512,1152]{1,0:T(8,128)(2,1)}, f32[512,1024]{1,0:T(8,128)}, bf16[512...) custom-call(bf16[512,1024]{1,0:T(8,128)(2,1)} %pad_maximum_fusion.3.n_ref, bf16[512,1024]{1,0:T(8,128)(2,1)} %copy-done.31, ...), custom_call_target="tpu_custom_call" | custom-call | flops 7247757312 | bytes 16777216 | tf_op jit(solution)/shard_map/pallas_call | solution.py:438
  227.8 13.8 %shard_map.250 = (bf16[512,1152]{1,0:T(8,128)(2,1)}, bf16[512,1152]{1,0:T(8,128)(2,1)}, bf16[512,1152]{1,0:T(8,128)(2,1)}, f32[512,1024]{1,0:T(8,128)}, bf16[512...) custom-call(bf16[512,1024]{1,0:T(8,128)(2,1)} %get-tuple-element.100.n_ref, bf16[512,1024]{1,0:T(8,128)(2,1)} %copy-done.7, ...), custom_call_target="tpu_custom_call" | custom-call | flops 7247757312 | bytes 16777216 | tf_op jit(solution)/shard_map/pallas_call | solution.py:438
  249.0 6.8 %shard_map.253 = (f32[512,1024]{1,0:T(8,128)}, bf16[512,1024]{1,0:T(8,128)(2,1)}, f32[1,1024]{1,0:T(1,128)}, bf16[2048,128]{1,0:T(8,128)(2,1)}) custom-call(s32[1]{0:T(128)} %bitcast.core_ref, bf16[512,1024]{1,0:T(8,128)(2,1)} %get-tuple-element.112.back_ref, bf16[512,1024]{1,0:T(8,128)(2,1)} %copy-done.60, bf16[256,1024]{1,0:T(8,128)(2,1)} %copy-done.77, ...), custom_call_target="tpu_custom_call" | custom-call | flops 536870912 | bytes 10485760 | tf_op jit(solution)/shard_map/pallas_call | solution.py:715
  255.8 5.5 %all-to-all-start.2 = ((bf16[16,128,128]{2,1,0:T(8,128)(2,1)}), bf16[16,128,128]{2,1,0:T(8,128)(2,1)}, u32[]{:S(2)}, u32[]{:S(2)}) async-start(bf16[16,128,128]{2,1,0:T(8,128)(2,1)} %bitcast.180), calls=%async_computation.2 | async-start | bytes 1048576 | tf_op jit(solution)/shard_map/all_to_all | solution.py:873
  263.5 14.6 %shard_map.254 = (bf16[512,1792]{1,0:T(8,128)(2,1)}, bf16[512,1792]{1,0:T(8,128)(2,1)}, bf16[512,1664]{1,0:T(8,128)(2,1)}, bf16[512,1664]{1,0:T(8,128)(2,1)}) custom-call(bf16[1024,512]{1,0:T(8,128)(2,1)} %get-tuple-element.116.refs_0_, bf16[1024,512]{1,0:T(8,128)(2,1)} %get-tuple-element.107.refs_1_, bf16[1024,512]{1,0:T(8,128)(2,1)} %get-tuple-element.117.refs_2_, ...), custom_call_target="tpu_custom_call" | custom-call | flops 7247757312 | bytes 16777216 | tf_op jit(solution)/shard_map/pallas_call | solution.py:516
  285.8 39.8 %shard_map.255 = (f32[4096,128]{1,0:T(8,128)}, f32[4096,128]{1,0:T(8,128)}, bf16[4096,128]{1,0:T(8,128)(2,1)}) custom-call(s32[1]{0:T(128)} %bitcast.core_ref, s32[32]{0:T(128)} %get-tuple-element.163.kslot_ref, s32[32]{0:T(128)} %get-tuple-element.162.qslot_ref, s32[4,8]{1,0:T(4,128)} %pad_add_fusion.lims_ref, bf16[4096,128]{1,0:T(8,128)(2,1)} %bitcast.66.q_ref.own_ref, ...), custom_call_target="tpu_custom_call" | custom-call | flops 17179869184 | bytes 8388608 | tf_op jit(solution)/shard_map/pallas_call | solution.py:361
  332.3 6.4 %shard_map.257 = bf16[1024,512]{1,0:T(8,128)(2,1)} custom-call(s32[1]{0:T(128)} %bitcast.core_ref, bf16[512,1024]{1,0:T(8,128)(2,1)} %get-tuple-element.136.attn_ref, bf16[512,1024]{1,0:T(8,128)(2,1)} %get-tuple-element.137.grad_ref, bf16[1024,1024]{1,0:T(8,128)(2,1)} %get-tuple-element.193.select_ref, bf16[1024,1024]{1,0:T(8,128)(2,1)} %get-tuple-element.111.unperm_ref), custom_call_target="tpu_custom_call" | custom-call | flops 4294967296 | bytes 8388608 | tf_op jit(solution)/shard_map/pallas_call | solution.py:475
  363.2 7.7 %all-to-all-done.3 = bf16[16,256,128]{2,1,0:T(8,128)(2,1)} async-done(((bf16[16,256,128]{2,1,0:T(8,128)(2,1)}), bf16[16,256,128]{2,1,0:T(8,128)(2,1)}, u32[]{:S(2)}, u32[]{:S(2)}) %all-to-all-start.3) | async-done | bytes 1048608 | tf_op jit(solution)/shard_map/all_to_all | solution.py:873
  370.9 7.3 %shard_map.256 = (bf16[512,1024]{1,0:T(8,128)(2,1)}, f32[8,8,128]{2,1,0:T(8,128)}) custom-call(s32[1]{0:T(128)} %bitcast.core_ref, bf16[8,2,256,128]{3,2,1,0:T(8,128)(2,1)} %bitcast.76.grad_ref, f32[512,1024]{1,0:T(8,128)} %get-tuple-element.132.raw_ref, f32[1,128]{1,0:T(1,128)} %maximum_bitcast_fusion.1.gain_ref, f32[256,128]{1,0:T(8,128)} %pad_maximum_fusion.25.cos_ref, ...), custom_call_target="tpu_custom_call" | custom-call | flops 16777216 | bytes 8388608 | tf_op jit(solution)/shard_map/pallas_call | solution.py:141
  389.5 9.7 %collective-permute-done.31 = bf16[512,768]{1,0:T(8,128)(2,1)S(1)} collective-permute-done((bf16[512,768]{1,0:T(8,128)(2,1)S(1)}, bf16[512,768]{1,0:T(8,128)(2,1)S(1)}, u32[]{:S(2)}, u32[]{:S(2)}) %collective-permute-start.31) | collective-permute-done | bytes 786464 | tf_op jit(solution)/shard_map/ppermute | solution.py:796
  413.6 5.3 %all-to-all-start.4 = ((f32[16,8,256]{2,1,0:T(8,128)}), f32[16,8,256]{2,1,0:T(8,128)S(1)}, u32[]{:S(2)}, u32[]{:S(2)}) async-start(f32[16,8,256]{2,1,0:T(8,128)} %broadcast_in_dim.174), calls=%async_computation.4 | async-start | bytes 262144 | tf_op jit(solution)/shard_map/all_to_all | solution.py:1157
  428.1 9.2 %collective-permute-done.43 = bf16[128,1664]{1,0:T(8,128)(2,1)} collective-permute-done((bf16[128,1664]{1,0:T(8,128)(2,1)}, bf16[128,1664]{1,0:T(8,128)(2,1)}, u32[]{:S(2)}, u32[]{:S(2)}) %collective-permute-start.43) | collective-permute-done | bytes 426016 | tf_op jit(solution)/shard_map/ppermute | solution.py:796
  438.6 8.4 %collective-permute-done.40 = bf16[128,1792]{1,0:T(8,128)(2,1)} collective-permute-done((bf16[128,1792]{1,0:T(8,128)(2,1)}, bf16[128,1792]{1,0:T(8,128)(2,1)}, u32[]{:S(2)}, u32[]{:S(2)}) %collective-permute-start.40) | collective-permute-done | bytes 458784 | tf_op jit(solution)/shard_map/ppermute | solution.py:796
  (471 shorter events, 226.7 us)
Async XLA Ops:
  5.2 23.8 %collective-permute-start.6 = (bf16[2,256,1024]{2,1,0:T(8,128)(2,1)}, bf16[2,256,1024]{2,1,0:T(8,128)(2,1)}, u32[]{:S(2)}, u32[]{:S(2)}) collective-permute-start(bf16[2,256,1024]{2,1,0:T(8,128)(2,1)} %pad_maximum_fusion.2), channel_id=1, source_target_pairs={{0,1},{1,0},{2,3},{3,2},{4,5},{5,4},{6,7},{7,6},{8,9},{9,8},{10,11... | collective-permute-start | bytes 3145736 | tf_op jit(solution)/shard_map/ppermute | solution.py:802
  48.4 31.8 %collective-permute-start.16 = (bf16[128,1664]{1,0:T(8,128)(2,1)S(1)}, bf16[128,1664]{1,0:T(8,128)(2,1)S(1)}, u32[]{:S(2)}, u32[]{:S(2)}) collective-permute-start(bf16[128,1664]{1,0:T(8,128)(2,1)S(1)} %maximum_select_fusion.11), channel_id=1, source_target_pairs={{0,16},{2,18},{4,20},{6,22},{8,24},{10,26},{12,28},{14,30},{16,0},... | collective-permute-start | bytes 1277960 | tf_op jit(solution)/shard_map/ppermute | solution.py:796
  49.6 39.2 %collective-permute-start.13 = (bf16[128,1792]{1,0:T(8,128)(2,1)S(1)}, bf16[128,1792]{1,0:T(8,128)(2,1)S(1)}, u32[]{:S(2)}, u32[]{:S(2)}) collective-permute-start(bf16[128,1792]{1,0:T(8,128)(2,1)S(1)} %maximum_select_fusion.10), channel_id=1, source_target_pairs={{0,16},{2,18},{4,20},{6,22},{8,24},{10,26},{12,28},{14,30},{16,0},... | collective-permute-start | bytes 1376264 | tf_op jit(solution)/shard_map/ppermute | solution.py:796
  66.0 36.0 %collective-permute-start.10 = (bf16[1024,512]{1,0:T(8,128)(2,1)}, bf16[1024,512]{1,0:T(8,128)(2,1)}, u32[]{:S(2)}, u32[]{:S(2)}) collective-permute-start(bf16[1024,512]{1,0:T(8,128)(2,1)} %maximum_maximum_fusion.1), channel_id=1, source_target_pairs={{0,1},{1,0},{2,3},{3,2},{4,5},{5,4},{6,7},{7,6},{8,9},{9,8},{10,11... | collective-permute-start | bytes 3145736 | tf_op jit(solution)/shard_map/ppermute | solution.py:802
  89.6 28.9 %all-to-all-start = ((bf16[16,256,128]{2,1,0:T(8,128)(2,1)}), bf16[16,256,128]{2,1,0:T(8,128)(2,1)}, u32[]{:S(2)}, u32[]{:S(2)}) async-start(bf16[16,256,128]{2,1,0:T(8,128)(2,1)} %bitcast.179), calls=%async_computation | async-start | bytes 2097152 | tf_op jit(solution)/shard_map/all_to_all | solution.py:873
  97.3 64.1 %collective-permute-start.17 = (bf16[256,1664]{1,0:T(8,128)(2,1)}, bf16[256,1664]{1,0:T(8,128)(2,1)}, u32[]{:S(2)}, u32[]{:S(2)}) collective-permute-start(bf16[256,1664]{1,0:T(8,128)(2,1)} %pad_maximum_fusion.10), channel_id=1, source_target_pairs={{0,4},{2,6},{4,0},{6,2},{8,12},{10,14},{12,8},{14,10},{16,20},{18,... | collective-permute-start | bytes 2555912 | tf_op jit(solution)/shard_map/ppermute | solution.py:796
  100.9 64.2 %collective-permute-start.14 = (bf16[256,1792]{1,0:T(8,128)(2,1)}, bf16[256,1792]{1,0:T(8,128)(2,1)}, u32[]{:S(2)}, u32[]{:S(2)}) collective-permute-start(bf16[256,1792]{1,0:T(8,128)(2,1)} %pad_maximum_fusion.6), channel_id=1, source_target_pairs={{0,8},{2,10},{4,12},{6,14},{8,0},{10,2},{12,4},{14,6},{16,24},{18,... | collective-permute-start | bytes 2752520 | tf_op jit(solution)/shard_map/ppermute | solution.py:796
  163.8 39.1 %collective-permute-start.18 = (bf16[512,1664]{1,0:T(8,128)(2,1)}, bf16[512,1664]{1,0:T(8,128)(2,1)}, u32[]{:S(2)}, u32[]{:S(2)}) collective-permute-start(bf16[512,1664]{1,0:T(8,128)(2,1)} %pad_maximum_fusion.1.refs_2_), channel_id=1, source_target_pairs={{0,8},{2,10},{4,12},{6,14},{8,0},{10,2},{12,4},{14,6},{16,24},{18,... | collective-permute-start | bytes 5111816 | tf_op jit(solution)/shard_map/ppermute | solution.py:796
  167.5 40.3 %collective-permute-start.15 = (bf16[512,1792]{1,0:T(8,128)(2,1)}, bf16[512,1792]{1,0:T(8,128)(2,1)}, u32[]{:S(2)}, u32[]{:S(2)}) collective-permute-start(bf16[512,1792]{1,0:T(8,128)(2,1)} %pad_maximum_fusion.refs_0_), channel_id=1, source_target_pairs={{0,4},{2,6},{4,0},{6,2},{8,12},{10,14},{12,8},{14,10},{16,20},{18,... | collective-permute-start | bytes 5505032 | tf_op jit(solution)/shard_map/ppermute | solution.py:796
  246.7 34.0 %collective-permute-start.23 = (bf16[512,1024]{1,0:T(8,128)(2,1)}, bf16[512,1024]{1,0:T(8,128)(2,1)}, u32[]{:S(2)}, u32[]{:S(2)}) collective-permute-start(bf16[512,1024]{1,0:T(8,128)(2,1)} %pad_maximum_fusion.4), channel_id=1, source_target_pairs={{0,1},{1,0},{2,3},{3,2},{4,5},{5,4},{6,7},{7,6},{8,9},{9,8},{10,11... | collective-permute-start | bytes 3145736 | tf_op jit(solution)/shard_map/ppermute | solution.py:802
  255.8 30.0 %all-to-all-start.2 = ((bf16[16,128,128]{2,1,0:T(8,128)(2,1)}), bf16[16,128,128]{2,1,0:T(8,128)(2,1)}, u32[]{:S(2)}, u32[]{:S(2)}) async-start(bf16[16,128,128]{2,1,0:T(8,128)(2,1)} %bitcast.180), calls=%async_computation.2 | async-start | bytes 1048576 | tf_op jit(solution)/shard_map/all_to_all | solution.py:873
  278.1 76.4 %collective-permute-start.41 = (bf16[512,1664]{1,0:T(8,128)(2,1)}, bf16[512,1664]{1,0:T(8,128)(2,1)}, u32[]{:S(2)}, u32[]{:S(2)}) collective-permute-start(bf16[512,1664]{1,0:T(8,128)(2,1)} %get-tuple-element.125), channel_id=1, source_target_pairs={{0,8},{2,10},{4,12},{6,14},{8,0},{10,2},{12,4},{14,6},{16,24},{18,... | collective-permute-start | bytes 5111816 | tf_op jit(solution)/shard_map/ppermute | solution.py:796
  279.6 79.3 %collective-permute-start.38 = (bf16[512,1792]{1,0:T(8,128)(2,1)}, bf16[512,1792]{1,0:T(8,128)(2,1)}, u32[]{:S(2)}, u32[]{:S(2)}) collective-permute-start(bf16[512,1792]{1,0:T(8,128)(2,1)} %get-tuple-element.124), channel_id=1, source_target_pairs={{0,4},{2,6},{4,0},{6,2},{8,12},{10,14},{12,8},{14,10},{16,20},{18,... | collective-permute-start | bytes 5505032 | tf_op jit(solution)/shard_map/ppermute | solution.py:796
  284.6 42.7 %collective-permute-start.24 = (bf16[256,1024]{1,0:T(8,128)(2,1)}, bf16[256,1024]{1,0:T(8,128)(2,1)}, u32[]{:S(2)}, u32[]{:S(2)}) collective-permute-start(bf16[256,1024]{1,0:T(8,128)(2,1)} %fusion.45), channel_id=1, source_target_pairs={{0,2},{2,0},{4,6},{6,4},{8,10},{10,8},{12,14},{14,12},{16,18},{18,... | collective-permute-start | bytes 1572872 | tf_op jit(solution)/shard_map/ppermute | solution.py:796
  343.1 27.8 %all-to-all-start.3 = ((bf16[16,256,128]{2,1,0:T(8,128)(2,1)}), bf16[16,256,128]{2,1,0:T(8,128)(2,1)}, u32[]{:S(2)}, u32[]{:S(2)}) async-start(bf16[16,256,128]{2,1,0:T(8,128)(2,1)} %bitcast.176), calls=%async_computation.3 | async-start | bytes 2097152 | tf_op jit(solution)/shard_map/all_to_all | solution.py:873
  357.7 45.5 %collective-permute-start.42 = (bf16[256,1664]{1,0:T(8,128)(2,1)}, bf16[256,1664]{1,0:T(8,128)(2,1)}, u32[]{:S(2)}, u32[]{:S(2)}) collective-permute-start(bf16[256,1664]{1,0:T(8,128)(2,1)} %get-tuple-element.169), channel_id=1, source_target_pairs={{0,4},{2,6},{4,0},{6,2},{8,12},{10,14},{12,8},{14,10},{16,20},{18,... | collective-permute-start | bytes 2555912 | tf_op jit(solution)/shard_map/ppermute | solution.py:796
  362.0 46.5 %collective-permute-start.39 = (bf16[256,1792]{1,0:T(8,128)(2,1)}, bf16[256,1792]{1,0:T(8,128)(2,1)}, u32[]{:S(2)}, u32[]{:S(2)}) collective-permute-start(bf16[256,1792]{1,0:T(8,128)(2,1)} %get-tuple-element.167), channel_id=1, source_target_pairs={{0,8},{2,10},{4,12},{6,14},{8,0},{10,2},{12,4},{14,6},{16,24},{18,... | collective-permute-start | bytes 2752520 | tf_op jit(solution)/shard_map/ppermute | solution.py:796
  387.1 23.3 %collective-permute-start.30 = (f32[256,1024]{1,0:T(8,128)S(1)}, f32[256,1024]{1,0:T(8,128)S(1)}, u32[]{:S(2)}, u32[]{:S(2)}) collective-permute-start(f32[256,1024]{1,0:T(8,128)S(1)} %slice_select_fusion.2), channel_id=1, source_target_pairs={{0,1},{1,0},{2,3},{3,2},{4,5},{5,4},{6,7},{7,6},{8,9},{9,8},{10,11... | collective-permute-start | bytes 3145736 | tf_op jit(solution)/shard_map/ppermute | solution.py:802
  400.2 22.9 %collective-permute-start.32 = (bf16[256,768]{1,0:T(8,128)(2,1)}, bf16[256,768]{1,0:T(8,128)(2,1)}, u32[]{:S(2)}, u32[]{:S(2)}) collective-permute-start(bf16[256,768]{1,0:T(8,128)(2,1)} %add_convert_fusion.12), channel_id=1, source_target_pairs={{0,2},{2,0},{4,6},{6,4},{8,10},{10,8},{12,14},{14,12},{16,18},{18,... | collective-permute-start | bytes 1179656 | tf_op jit(solution)/shard_map/ppermute | solution.py:796
  402.6 21.8 %collective-permute-start.34 = (bf16[256,768]{1,0:T(8,128)(2,1)}, bf16[256,768]{1,0:T(8,128)(2,1)}, u32[]{:S(2)}, u32[]{:S(2)}) collective-permute-start(bf16[256,768]{1,0:T(8,128)(2,1)} %add_convert_fusion.10), channel_id=1, source_target_pairs={{0,4},{2,6},{4,0},{6,2},{8,12},{10,14},{12,8},{14,10},{16,20},{18,... | collective-permute-start | bytes 1179656 | tf_op jit(solution)/shard_map/ppermute | solution.py:796
  405.0 32.2 %collective-permute-start.43 = (bf16[128,1664]{1,0:T(8,128)(2,1)}, bf16[128,1664]{1,0:T(8,128)(2,1)}, u32[]{:S(2)}, u32[]{:S(2)}) collective-permute-start(bf16[128,1664]{1,0:T(8,128)(2,1)} %add_convert_fusion.8), channel_id=1, source_target_pairs={{0,16},{2,18},{4,20},{6,22},{8,24},{10,26},{12,28},{14,30},{16,0},... | collective-permute-start | bytes 1277960 | tf_op jit(solution)/shard_map/ppermute | solution.py:796
  410.4 36.7 %collective-permute-start.40 = (bf16[128,1792]{1,0:T(8,128)(2,1)}, bf16[128,1792]{1,0:T(8,128)(2,1)}, u32[]{:S(2)}, u32[]{:S(2)}) collective-permute-start(bf16[128,1792]{1,0:T(8,128)(2,1)} %add_convert_fusion.6), channel_id=1, source_target_pairs={{0,16},{2,18},{4,20},{6,22},{8,24},{10,26},{12,28},{14,30},{16,0},... | collective-permute-start | bytes 1376264 | tf_op jit(solution)/shard_map/ppermute | solution.py:796
  413.6 35.2 %all-to-all-start.4 = ((f32[16,8,256]{2,1,0:T(8,128)}), f32[16,8,256]{2,1,0:T(8,128)S(1)}, u32[]{:S(2)}, u32[]{:S(2)}) async-start(f32[16,8,256]{2,1,0:T(8,128)} %broadcast_in_dim.174), calls=%async_computation.4 | async-start | bytes 262144 | tf_op jit(solution)/shard_map/all_to_all | solution.py:1157
  426.6 27.9 %collective-permute-start.35 = (bf16[128,1536]{1,0:T(8,128)(2,1)}, bf16[128,1536]{1,0:T(8,128)(2,1)}, u32[]{:S(2)}, u32[]{:S(2)}) collective-permute-start(bf16[128,1536]{1,0:T(8,128)(2,1)} %fusion.75), channel_id=1, source_target_pairs={{0,8},{2,10},{4,12},{6,14},{8,0},{10,2},{12,4},{14,6},{16,24},{18,... | collective-permute-start | bytes 1179656 | tf_op jit(solution)/shard_map/ppermute | solution.py:796
  (131 other events, 1105.6 us)
